TPU v7x, 128 devices: a whole 4x4x4 slice. The times are simulated.
128 devices in a mesh: ctx: 8 (over y, core), tp: 8 (over x, z_hi), dp: 2 (over z_lo).
Axes of the slice: x: 4, y: 4, z: 4 (z_hi: 2, z_lo: 2; z = z_hi * 2 + z_lo), core: 2. Of those that a mesh axis runs over, the one named last changes fastest.
Arguments:
- signal_first: bfloat16 [131072, 128], P(('ctx', 'tp', 'dp')), may hold values from -6 to 6
- gate_first: bfloat16 [131072, 128], P(('ctx', 'tp', 'dp')), may hold values from -6 to 6
- signal_second: bfloat16 [131072, 128], P(('ctx', 'tp', 'dp')), may hold values from -6 to 6
- gate_second: bfloat16 [131072, 128], P(('ctx', 'tp', 'dp')), may hold values from -6 to 6
- upstream_second: bfloat16 [131072, 128], P(('ctx', 'tp', 'dp')), may hold values from -6 to 6
- filter_param: bfloat16 [131072, 128], P(('ctx', 'tp', 'dp')), may hold values from -6 to 6
Outputs:
- mixed_first: bfloat16 [131072, 128], P(('ctx', 'tp', 'dp'))
- signal_grad: bfloat16 [131072, 128], P(('ctx', 'tp', 'dp'))
- gate_grad: bfloat16 [131072, 128], P(('ctx', 'tp', 'dp'))
- filter_grad: float32 [131072, 128], P(('ctx', 'tp', 'dp'))
All inputs are finite; a program needn't handle non-finite values.
Results may differ from a plain program's by a relative error of at most 0.0049.
Values may be sent and summed in bfloat16 or wider, within the bound.
No kernel may reach another device: no remote copies, remote signals or barrier semaphores. Data moves between devices by JAX's collectives and lax.ppermute only.
A program may use at most 128 MiB of HBM per device.

v0:
```python
import math

import jax
import jax.numpy as jnp
from jax import lax
from jax.sharding import PartitionSpec as P

FA = 512
FB = 512
SEQ = 131072


HIGHEST = lax.Precision.HIGHEST
TWO_PI = 2.0 * math.pi


def phase_table(row_index, col_index, period):
    product = row_index[:, None] * col_index[None, :] % period
    return TWO_PI * product.astype(jnp.float32) / period


def spread_input(values):
    return lax.all_to_all(values, ("ctx", "tp", "dp"), split_axis=2, concat_axis=1, tiled=True)


def spectrum_rows(values):
    return lax.all_to_all(values, ("ctx", "tp", "dp"), split_axis=1, concat_axis=2, tiled=True)


def inverse_columns(values):
    return lax.all_to_all(values, ("ctx", "tp", "dp"), split_axis=2, concat_axis=1, tiled=True)


def output_rows(values):
    return lax.all_to_all(values, ("ctx", "tp", "dp"), split_axis=1, concat_axis=2, tiled=True)


def apply_second(values, table):
    return jnp.einsum("rbc,bj->rjc", values, table, precision=HIGHEST)


def frequency_order(devices):
    pair_index = jnp.arange(FA // 2, dtype=jnp.int32).reshape((devices, FA // (2 * devices)))
    upper = jnp.where(pair_index == 0, FA // 2, FA - pair_index)
    return jnp.concatenate([pair_index, upper], axis=1).reshape((FA,))


def make_tables(freq_all, col_global, row_global):
    period = FA * FB
    half_index = jnp.arange(FA // 2, dtype=jnp.int32)
    second_index = jnp.arange(FB, dtype=jnp.int32)
    first_phase = phase_table(freq_all, half_index, FA)
    second_phase = phase_table(second_index, second_index, FB)
    twist_fwd = phase_table(freq_all, col_global, period)[:, :, None]
    twist_back = phase_table(row_global, second_index, period)[:, :, None]
    return (
        jnp.cos(first_phase),
        jnp.sin(first_phase),
        jnp.cos(second_phase),
        jnp.sin(second_phase),
        jnp.cos(twist_fwd),
        jnp.sin(twist_fwd),
        jnp.cos(twist_back),
        jnp.sin(twist_back),
    )


def forward(arrived, tables):
    cos_first, sin_first, cos_second, sin_second, cos_fwd, sin_fwd, cos_back, sin_back = tables
    values = arrived.astype(jnp.float32)
    cos_real = jnp.einsum("ka,abc->kbc", cos_first, values[0], precision=HIGHEST)
    sin_real = jnp.einsum("ka,abc->kbc", sin_first, values[0], precision=HIGHEST)
    imag_part = -sin_real
    turned = jnp.stack(
        [cos_real * cos_fwd + imag_part * sin_fwd, imag_part * cos_fwd - cos_real * sin_fwd]
    )
    arrived_rows = spectrum_rows(turned)
    spec_real = apply_second(arrived_rows[0], cos_second) + apply_second(
        arrived_rows[1], sin_second
    )
    spec_imag = apply_second(arrived_rows[1], cos_second) - apply_second(
        arrived_rows[0], sin_second
    )
    return (spec_real, spec_imag)


def inverse(spec_real, spec_imag, tables):
    cos_first, sin_first, cos_second, sin_second, cos_fwd, sin_fwd, cos_back, sin_back = tables
    back_real = apply_second(spec_real, cos_second) - apply_second(spec_imag, sin_second)
    back_imag = apply_second(spec_real, sin_second) + apply_second(spec_imag, cos_second)
    turned = jnp.stack(
        [back_real * cos_back - back_imag * sin_back, back_real * sin_back + back_imag * cos_back]
    )
    arrived = inverse_columns(turned)
    real_out = jnp.einsum("ka,kbc->abc", cos_first, arrived[0], precision=HIGHEST)
    real_out = real_out - jnp.einsum("ka,kbc->abc", sin_first, arrived[1], precision=HIGHEST)
    summed = real_out[None]
    return output_rows(summed / (FA * FB))


def spectral_products(spectra):
    gain_scale = 1.0 / math.sqrt(SEQ)
    first_real, first_imag = spectra[0]
    second_real, second_imag = spectra[1]
    middle_real, middle_imag = spectra[2]
    filter_real = gain_scale * spectra[3][0]
    filter_imag = gain_scale * spectra[3][1]
    return [
        (
            filter_real * first_real - filter_imag * first_imag,
            filter_real * first_imag + filter_imag * first_real,
        ),
        (
            filter_real * second_real - filter_imag * second_imag,
            filter_real * second_imag + filter_imag * second_real,
        ),
        (
            filter_real * middle_real + filter_imag * middle_imag,
            filter_real * middle_imag - filter_imag * middle_real,
        ),
        (
            gain_scale * (middle_real * second_real + middle_imag * second_imag),
            gain_scale * (middle_imag * second_real - middle_real * second_imag),
        ),
    ]


def on_device(signal_first, gate_first, signal_second, gate_second, upstream_second, filter_param):
    local_len = signal_first.shape[0]
    channels = signal_first.shape[1]
    devices = lax.axis_size(("ctx", "tp", "dp"))
    device_rank = lax.axis_index(("ctx", "tp", "dp"))
    grad_mid = (gate_second.astype(jnp.float32) * upstream_second.astype(jnp.float32)).astype(
        jnp.bfloat16
    )
    rows_local = FA // 2 // devices
    cols_local = FB // devices
    spec_rows = FA // devices
    freq_all = frequency_order(devices)
    row_global = lax.dynamic_slice_in_dim(freq_all, device_rank * spec_rows, spec_rows)
    col_global = device_rank * cols_local + jnp.arange(cols_local, dtype=jnp.int32)
    tables = make_tables(freq_all, col_global, row_global)

    def to_tiles(values):
        return values.reshape((1, rows_local, FB, channels))

    def run_inverse(spectra_list):
        return [inverse(element[0], element[1], tables) for element in spectra_list]

    tiles = [
        to_tiles(signal_first),
        to_tiles(signal_second),
        to_tiles(grad_mid),
        to_tiles(filter_param),
    ]
    spectra = [forward(spread_input(group), tables) for group in tiles]
    products = spectral_products(spectra)
    outputs = run_inverse(products)
    results = [element[0] for element in outputs]
    results = [element.reshape((local_len, channels)) for element in results]
    mixed_first = (gate_first.astype(jnp.float32) * results[0]).astype(jnp.bfloat16)
    gate_grad = (upstream_second.astype(jnp.float32) * results[1]).astype(jnp.bfloat16)
    signal_grad = results[2].astype(jnp.bfloat16)
    filter_grad = results[3]
    return (mixed_first, signal_grad, gate_grad, filter_grad)


def solution(mesh):
    return jax.shard_map(
        on_device,
        mesh=mesh,
        in_specs=(
            P(("ctx", "tp", "dp"), None),
            P(("ctx", "tp", "dp"), None),
            P(("ctx", "tp", "dp"), None),
            P(("ctx", "tp", "dp"), None),
            P(("ctx", "tp", "dp"), None),
            P(("ctx", "tp", "dp"), None),
        ),
        out_specs=(
            P(("ctx", "tp", "dp"), None),
            P(("ctx", "tp", "dp"), None),
            P(("ctx", "tp", "dp"), None),
            P(("ctx", "tp", "dp"), None),
        ),
        check_vma=False,
    )
```

profile of v0, /device:TPU:0, one launch (start us, length us, event | category | flops | bytes accessed | tf_op | source)
XLA Modules:
  0.0 612.3 jit_solution(10912970498057550036)
XLA Ops:
  2.8 11.1 %all-to-all-start.6 = ((bf16[1,2,512,128]{3,1,0,2:T(2,128)(2,1)}), bf16[1,2,512,128]{3,1,0,2:T(2,128)(2,1)S(1)}, u32[]{:S(2)}, u32[]{:S(2)}) async-start(bf16[1,2,512,128]{3,1,0,2:T(2,128)(2,1)} %copy.130), calls=%async_computation.6 | async-start | bytes 524288 | tf_op jit(solution)/shard_map/all_to_all | solution.py:23
  17.3 7.5 %all-to-all-done.6 = bf16[1,2,512,128]{3,1,0,2:T(2,128)(2,1)S(1)} async-done(((bf16[1,2,512,128]{3,1,0,2:T(2,128)(2,1)}), bf16[1,2,512,128]{3,1,0,2:T(2,128)(2,1)S(1)}, u32[]{:S(2)}, u32[]{:S(2)}) %all-to-all-start.6) | async-done | bytes 262176 | tf_op jit(solution)/shard_map/all_to_all | solution.py:23
  56.3 6.4 %all-to-all-start = ((bf16[1,2,512,128]{3,1,0,2:T(2,128)(2,1)}), bf16[1,2,512,128]{3,1,0,2:T(2,128)(2,1)S(1)}, u32[]{:S(2)}, u32[]{:S(2)}) async-start(bf16[1,2,512,128]{3,1,0,2:T(2,128)(2,1)} %copy.112), calls=%async_computation | async-start | bytes 524288 | tf_op jit(solution)/shard_map/all_to_all | solution.py:23
  76.5 6.3 %add_bitcast_fusion.2 = (f32[1,512,4,128]{3,1,2,0:T(8,128)}, f32[1,512,4,128]{3,1,2,0:T(8,128)}, f32[1,512,4,128]{3,1,2,0:T(8,128)S(1)}, f32[1,512,4,128]{3,1,2,...) fusion(f32[512,4,128]{2,0,1:T(8,128)} %convolution_negate_fusio, ...), kind=kOutput, calls=%fused_computation.137 | convolution fusion | flops 813432832 | bytes 16009216 | tf_op jit(solution)/shard_map/ka,abc->kbc/dot_general | solution.py:71
  85.6 6.2 %all-to-all-start.3 = ((f32[2,512,4,128]{3,2,0,1:T(4,128)}), f32[2,512,4,128]{3,2,0,1:T(4,128)S(1)}, u32[]{:S(2)}, u32[]{:S(2)}) async-start(f32[2,512,4,128]{3,2,0,1:T(4,128)} %copy.124), calls=%async_computation.3 | async-start | bytes 4194304 | tf_op jit(solution)/shard_map/all_to_all | solution.py:27
  96.2 25.3 %all-to-all-done.3 = f32[2,512,4,128]{3,2,0,1:T(4,128)S(1)} async-done(((f32[2,512,4,128]{3,2,0,1:T(4,128)}), f32[2,512,4,128]{3,2,0,1:T(4,128)S(1)}, u32[]{:S(2)}, u32[]{:S(2)}) %all-to-all-start.3) | async-done | bytes 2097184 | tf_op jit(solution)/shard_map/all_to_all | solution.py:27
  121.5 5.8 all-to-all-start.1
  131.7 24.9 %all-to-all-done.1 = f32[2,512,4,128]{3,2,0,1:T(4,128)} async-done(((f32[2,512,4,128]{3,2,0,1:T(4,128)}), f32[2,512,4,128]{3,2,0,1:T(4,128)}, u32[]{:S(2)}, u32[]{:S(2)}) %all-to-all-start.1) | async-done | bytes 2097184 | tf_op jit(solution)/shard_map/all_to_all | solution.py:27
  156.6 6.0 all-to-all-start.11
  169.4 7.0 %fusion.81 = f32[512,4,128]{2,0,1:T(8,128)} fusion(f32[4,512,128]{2,1,0:T(8,128)S(1)} %bitcast.359), kind=kOutput, calls=%fused_computation.124 | convolution fusion | flops 1614282752 | bytes 2097152 | tf_op jit(solution)/shard_map/rbc,bj->rjc/dot_general | solution.py:39
  176.4 7.0 %fusion.77 = f32[512,4,128]{2,0,1:T(8,128)} fusion(f32[4,512,128]{2,1,0:T(8,128)S(1)} %bitcast.363), kind=kOutput, calls=%fused_computation.120 | convolution fusion | flops 1614282752 | bytes 2097152 | tf_op jit(solution)/shard_map/rbc,bj->rjc/dot_general | solution.py:39
  184.5 7.0 %fusion.83 = f32[512,4,128]{2,0,1:T(8,128)} fusion(f32[4,512,128]{2,1,0:T(8,128)S(1)} %bitcast.361), kind=kOutput, calls=%fused_computation.126 | convolution fusion | flops 1614282752 | bytes 2097152 | tf_op jit(solution)/shard_map/rbc,bj->rjc/dot_general | solution.py:39
  191.8 9.9 %all-to-all-start.7 = ((f32[2,512,4,128]{3,2,0,1:T(4,128)}), f32[2,512,4,128]{3,2,0,1:T(4,128)S(1)}, u32[]{:S(2)}, u32[]{:S(2)}) async-start(f32[2,512,4,128]{3,2,0,1:T(4,128)} %copy.135), calls=%async_computation.7 | async-start | bytes 4194304 | tf_op jit(solution)/shard_map/all_to_all | solution.py:27
  209.6 5.9 fusion.67
  215.5 7.0 %fusion.65 = f32[512,4,128]{2,0,1:T(8,128)} fusion(f32[4,512,128]{2,1,0:T(8,128)S(1)} %bitcast.367), kind=kOutput, calls=%fused_computation.108 | convolution fusion | flops 1614282752 | bytes 2097152 | tf_op jit(solution)/shard_map/rbc,bj->rjc/dot_general | solution.py:39
  222.5 5.7 convolution_add_fusion.6
  228.3 7.0 %convolution_subtract_fusion.6 = f32[512,4,128]{2,0,1:T(8,128)} fusion(f32[512,4,128]{2,0,1:T(8,128)S(1)} %copy-done.24, f32[4,512,128]{2,1,0:T(8,128)S(1)} %bitcast.360), kind=kOutput, calls=%fused_computation.41 | convolution fusion | flops 1614544896 | bytes 3145728 | tf_op jit(solution)/shard_map/rbc,bj->rjc/dot_general | solution.py:39
  235.3 7.2 %fusion.9 = f32[512,4,128]{2,0,1:T(8,128)} fusion(f32[512,4,128]{2,0,1:T(8,128)S(1)} %copy-done.26, f32[4,512,128]{2,1,0:T(8,128)S(1)} %bitcast.366), kind=kOutput, calls=%fused_computation.47 | convolution fusion | flops 1614807040 | bytes 3145728 | tf_op jit(solution)/shard_map/rbc,bj->rjc/dot_general | solution.py:39
  242.6 7.0 %fusion.8 = f32[512,4,128]{2,0,1:T(8,128)} fusion(f32[512,4,128]{2,0,1:T(8,128)S(1)} %fusion.79, f32[4,512,128]{2,1,0:T(8,128)S(1)} %bitcast.362), kind=kOutput, calls=%fused_computation.43 | convolution fusion | flops 1614807040 | bytes 3145728 | tf_op jit(solution)/shard_map/rbc,bj->rjc/dot_general | solution.py:39
  249.6 7.4 %convolution_add_fusion.2 = f32[512,4,128]{2,0,1:T(8,128)} fusion(f32[512,4,128]{2,0,1:T(8,128)S(1)} %fusion.67, f32[4,512,128]{2,1,0:T(8,128)S(1)} %bitcast.368), kind=kOutput, calls=%fused_computation.28 | convolution fusion | flops 1614544896 | bytes 3145728 | tf_op jit(solution)/shard_map/rbc,bj->rjc/dot_general | solution.py:39
  257.5 5.7 fusion.71
  263.2 5.9 fusion.73
  269.1 5.7 convolution_subtract_fusion.4
  274.9 5.7 convolution_subtract_fusion.2
  280.7 7.2 %subtract_multiply_fusion = (f32[512,4,128]{2,0,1:T(8,128)S(1)}, f32[512,4,128]{2,0,1:T(8,128)S(1)}, f32[512,4,128]{2,0,1:T(8,128)S(1)}, f32[512,4,128]{2,0,1:T(...) fusion(f32[512,4,128]{2,0,1:T(8,128)S(1)} %convolution_subtract, ...), kind=kOutput, calls=%fused_computation.130 | convolution fusion | flops 1621360640 | bytes 17825792 | tf_op jit(solution)/shard_map/rbc,bj->rjc/dot_general | solution.py:39
  293.6 6.1 %fusion.29 = f32[512,4,128]{2,0,1:T(8,128)S(1)} fusion(f32[512,4,128]{2,0,1:T(8,128)S(1)} %get-tuple-element.30), kind=kOutput, calls=%fused_computation.72 | convolution fusion | flops 1614282752 | bytes 2097152 | tf_op jit(solution)/shard_map/rbc,bj->rjc/dot_general | solution.py:39
  305.4 5.9 fusion.35
  317.1 5.9 fusion.23
  323.0 5.7 fusion.41
  328.7 6.1 fusion.43
  334.8 5.8 fusion.3
  340.6 5.9 fusion.2
  346.5 5.7 fusion.5
  352.2 5.9 fusion.4
  358.1 5.8 fusion.1
  363.9 6.1 fusion
  375.7 9.0 %subtract_bitcast_fusion = (f32[1,4,512,128]{3,2,1,0:T(8,128)S(1)}, f32[1,4,512,128]{3,2,1,0:T(8,128)S(1)}, f32[1,4,512,128]{3,2,1,0:T(8,128)}, f32[1,4,512,128]...) fusion(f32[4,512,128]{2,1,0:T(8,128)S(1)} %fusion, ...), kind=kOutput, calls=%fused_computation.129 | convolution fusion | flops 1620836352 | bytes 17842176 | tf_op jit(solution)/shard_map/rbc,bj->rjc/dot_general | solution.py:39
  387.5 9.9 %all-to-all-start.14 = ((f32[2,4,512,128]{3,1,0,2:T(4,128)}), f32[2,4,512,128]{3,1,0,2:T(4,128)S(1)}, u32[]{:S(2)}, u32[]{:S(2)}) async-start(f32[2,4,512,128]{3,1,0,2:T(4,128)} %copy.152), calls=%async_computation.14 | async-start | bytes 4194304 | tf_op jit(solution)/shard_map/all_to_all | solution.py:31
  401.8 25.3 %all-to-all-done.14 = f32[2,4,512,128]{3,1,0,2:T(4,128)S(1)} async-done(((f32[2,4,512,128]{3,1,0,2:T(4,128)}), f32[2,4,512,128]{3,1,0,2:T(4,128)S(1)}, u32[]{:S(2)}, u32[]{:S(2)}) %all-to-all-start.14) | async-done | bytes 2097184 | tf_op jit(solution)/shard_map/all_to_all | solution.py:31
  437.5 25.3 %all-to-all-done.12 = f32[2,4,512,128]{3,1,0,2:T(4,128)S(1)} async-done(((f32[2,4,512,128]{3,1,0,2:T(4,128)}), f32[2,4,512,128]{3,1,0,2:T(4,128)S(1)}, u32[]{:S(2)}, u32[]{:S(2)}) %all-to-all-start.12) | async-done | bytes 2097184 | tf_op jit(solution)/shard_map/all_to_all | solution.py:31
  462.8 5.8 all-to-all-start.8
  472.7 25.2 %all-to-all-done.8 = f32[2,4,512,128]{3,1,0,2:T(4,128)} async-done(((f32[2,4,512,128]{3,1,0,2:T(4,128)}), f32[2,4,512,128]{3,1,0,2:T(4,128)}, u32[]{:S(2)}, u32[]{:S(2)}) %all-to-all-start.8) | async-done | bytes 2097184 | tf_op jit(solution)/shard_map/all_to_all | solution.py:31
  497.9 6.0 all-to-all-start.4
  516.1 17.0 %all-to-all-done.4 = f32[2,4,512,128]{3,1,0,2:T(4,128)} async-done(((f32[2,4,512,128]{3,1,0,2:T(4,128)}), f32[2,4,512,128]{3,1,0,2:T(4,128)}, u32[]{:S(2)}, u32[]{:S(2)}) %all-to-all-start.4) | async-done | bytes 2097184 | tf_op jit(solution)/shard_map/all_to_all | solution.py:31
  548.9 9.6 %all-to-all-start.15 = ((f32[1,256,4,128]{3,2,0,1:T(4,128)}), f32[1,256,4,128]{3,2,0,1:T(4,128)S(1)}, u32[]{:S(2)}, u32[]{:S(2)}) async-start(f32[1,256,4,128]{3,2,0,1:T(4,128)} %copy.154), calls=%async_computation.15 | async-start | bytes 1048576 | tf_op jit(solution)/shard_map/all_to_all | solution.py:35
  572.1 7.3 %all-to-all-start.13 = ((f32[1,256,4,128]{3,2,0,1:T(4,128)}), f32[1,256,4,128]{3,2,0,1:T(4,128)S(1)}, u32[]{:S(2)}, u32[]{:S(2)}) async-start(f32[1,256,4,128]{3,2,0,1:T(4,128)} %copy.150), calls=%async_computation.13 | async-start | bytes 1048576 | tf_op jit(solution)/shard_map/all_to_all | solution.py:35
  586.8 6.3 %all-to-all-done.13 = f32[1,256,4,128]{3,2,0,1:T(4,128)S(1)} async-done(((f32[1,256,4,128]{3,2,0,1:T(4,128)}), f32[1,256,4,128]{3,2,0,1:T(4,128)S(1)}, u32[]{:S(2)}, u32[]{:S(2)}) %all-to-all-start.13) | async-done | bytes 524320 | tf_op jit(solution)/shard_map/all_to_all | solution.py:35
  600.2 11.1 %all-to-all-done.5 = f32[1,256,4,128]{3,2,0,1:T(4,128)S(1)} async-done(((f32[1,256,4,128]{3,2,0,1:T(4,128)}), f32[1,256,4,128]{3,2,0,1:T(4,128)S(1)}, u32[]{:S(2)}, u32[]{:S(2)}) %all-to-all-start.5) | async-done | bytes 524320 | tf_op jit(solution)/shard_map/all_to_all | solution.py:35
  (149 shorter events, 180.0 us)
Async XLA Ops:
  0.6 13.6 %copy-start.19 = (bf16[1024,128]{1,0:T(8,128)(2,1)S(1)}, bf16[1024,128]{1,0:T(8,128)(2,1)}, u32[]{:S(2)}) copy-start(bf16[1024,128]{1,0:T(8,128)(2,1)} %param.6) | copy-start | bytes 786436
  0.6 14.6 %copy-start.20 = (bf16[1024,128]{1,0:T(8,128)(2,1)S(1)}, bf16[1024,128]{1,0:T(8,128)(2,1)}, u32[]{:S(2)}) copy-start(bf16[1024,128]{1,0:T(8,128)(2,1)} %param.11) | copy-start | bytes 786436
  0.7 15.5 %copy-start.21 = (bf16[1024,128]{1,0:T(8,128)(2,1)S(1)}, bf16[1024,128]{1,0:T(8,128)(2,1)}, u32[]{:S(2)}) copy-start(bf16[1024,128]{1,0:T(8,128)(2,1)} %param.8) | copy-start | bytes 786436
  2.8 22.0 %all-to-all-start.6 = ((bf16[1,2,512,128]{3,1,0,2:T(2,128)(2,1)}), bf16[1,2,512,128]{3,1,0,2:T(2,128)(2,1)S(1)}, u32[]{:S(2)}, u32[]{:S(2)}) async-start(bf16[1,2,512,128]{3,1,0,2:T(2,128)(2,1)} %copy.130), calls=%async_computation.6 | async-start | bytes 524288 | tf_op jit(solution)/shard_map/all_to_all | solution.py:23
  24.8 15.5 %all-to-all-start.2 = ((bf16[1,2,512,128]{3,1,0,2:T(2,128)(2,1)}), bf16[1,2,512,128]{3,1,0,2:T(2,128)(2,1)S(1)}, u32[]{:S(2)}, u32[]{:S(2)}) async-start(bf16[1,2,512,128]{3,1,0,2:T(2,128)(2,1)} %copy.119), calls=%async_computation.2 | async-start | bytes 524288 | tf_op jit(solution)/shard_map/all_to_all | solution.py:23
  40.4 16.0 %all-to-all-start.10 = ((bf16[1,2,512,128]{3,1,0,2:T(2,128)(2,1)}), bf16[1,2,512,128]{3,1,0,2:T(2,128)(2,1)S(1)}, u32[]{:S(2)}, u32[]{:S(2)}) async-start(bf16[1,2,512,128]{3,1,0,2:T(2,128)(2,1)} %copy.141), calls=%async_computation.10 | async-start | bytes 524288 | tf_op jit(solution)/shard_map/all_to_all | solution.py:23
  56.3 17.3 %all-to-all-start = ((bf16[1,2,512,128]{3,1,0,2:T(2,128)(2,1)}), bf16[1,2,512,128]{3,1,0,2:T(2,128)(2,1)S(1)}, u32[]{:S(2)}, u32[]{:S(2)}) async-start(bf16[1,2,512,128]{3,1,0,2:T(2,128)(2,1)} %copy.112), calls=%async_computation | async-start | bytes 524288 | tf_op jit(solution)/shard_map/all_to_all | solution.py:23
  73.6 2.8 copy-start.1
  73.6 2.8 copy-start.2
  73.6 2.8 copy-start.7
  85.6 36.0 %all-to-all-start.3 = ((f32[2,512,4,128]{3,2,0,1:T(4,128)}), f32[2,512,4,128]{3,2,0,1:T(4,128)S(1)}, u32[]{:S(2)}, u32[]{:S(2)}) async-start(f32[2,512,4,128]{3,2,0,1:T(4,128)} %copy.124), calls=%async_computation.3 | async-start | bytes 4194304 | tf_op jit(solution)/shard_map/all_to_all | solution.py:27
  121.5 35.1 %all-to-all-start.1 = ((f32[2,512,4,128]{3,2,0,1:T(4,128)}), f32[2,512,4,128]{3,2,0,1:T(4,128)}, u32[]{:S(2)}, u32[]{:S(2)}) async-start(f32[2,512,4,128]{3,2,0,1:T(4,128)} %copy.117), calls=%async_computation.1 | async-start | bytes 4194304 | tf_op jit(solution)/shard_map/all_to_all | solution.py:27
  156.6 35.2 %all-to-all-start.11 = ((f32[2,512,4,128]{3,2,0,1:T(4,128)}), f32[2,512,4,128]{3,2,0,1:T(4,128)}, u32[]{:S(2)}, u32[]{:S(2)}) async-start(f32[2,512,4,128]{3,2,0,1:T(4,128)} %copy.146), calls=%async_computation.11 | async-start | bytes 4194304 | tf_op jit(solution)/shard_map/all_to_all | solution.py:27
  169.4 7.0 %copy-start.11 = (f32[1,4,128,4,128]{4,3,2,1,0:T(4,128)}, f32[1,4,128,4,128]{4,3,2,1,0:T(4,128)S(1)}, u32[]{:S(2)}) copy-start(f32[1,4,128,4,128]{4,3,2,1,0:T(4,128)S(1)} %get-tuple-element.46) | copy-start | bytes 3145732
  169.4 7.0 %copy-start.15 = (f32[1,4,128,4,128]{4,3,2,1,0:T(4,128)}, f32[1,4,128,4,128]{4,3,2,1,0:T(4,128)S(1)}, u32[]{:S(2)}) copy-start(f32[1,4,128,4,128]{4,3,2,1,0:T(4,128)S(1)} %get-tuple-element.47) | copy-start | bytes 3145732
  183.5 1.0 copy-start.13
  183.5 20.4 %copy-start.17 = (f32[1,4,128,4,128]{4,3,2,1,0:T(4,128)}, f32[1,4,128,4,128]{4,3,2,1,0:T(4,128)S(1)}, u32[]{:S(2)}) copy-start(f32[1,4,128,4,128]{4,3,2,1,0:T(4,128)S(1)} %get-tuple-element.49) | copy-start | bytes 3145732
  191.8 65.1 %all-to-all-start.7 = ((f32[2,512,4,128]{3,2,0,1:T(4,128)}), f32[2,512,4,128]{3,2,0,1:T(4,128)S(1)}, u32[]{:S(2)}, u32[]{:S(2)}) async-start(f32[2,512,4,128]{3,2,0,1:T(4,128)} %copy.135), calls=%async_computation.7 | async-start | bytes 4194304 | tf_op jit(solution)/shard_map/all_to_all | solution.py:27
  203.9 5.7 copy-start.9
  215.5 7.0 %copy-start.16 = (f32[1,4,128,4,128]{4,3,2,1,0:T(4,128)S(1)}, f32[1,4,128,4,128]{4,3,2,1,0:T(4,128)}, u32[]{:S(2)}) copy-start(f32[1,4,128,4,128]{4,3,2,1,0:T(4,128)} %copy-done.15) | copy-start | bytes 3145732
  215.5 7.0 %copy-start.25 = (f32[512,4,128]{2,0,1:T(8,128)S(1)}, f32[512,4,128]{2,0,1:T(8,128)}, u32[]{:S(2)}) copy-start(f32[512,4,128]{2,0,1:T(8,128)} %fusion.81) | copy-start | bytes 3145732
  222.5 5.7 copy-start.12
  222.5 5.8 copy-start.24
  228.3 7.1 %copy-start.18 = (f32[1,4,128,4,128]{4,3,2,1,0:T(4,128)S(1)}, f32[1,4,128,4,128]{4,3,2,1,0:T(4,128)}, u32[]{:S(2)}) copy-start(f32[1,4,128,4,128]{4,3,2,1,0:T(4,128)} %copy-done.17) | copy-start | bytes 3145732
  228.3 7.1 %copy-start.26 = (f32[512,4,128]{2,0,1:T(8,128)S(1)}, f32[512,4,128]{2,0,1:T(8,128)}, u32[]{:S(2)}) copy-start(f32[512,4,128]{2,0,1:T(8,128)} %fusion.83) | copy-start | bytes 3145732
  235.3 7.2 %copy-start.14 = (f32[1,4,128,4,128]{4,3,2,1,0:T(4,128)S(1)}, f32[1,4,128,4,128]{4,3,2,1,0:T(4,128)}, u32[]{:S(2)}) copy-start(f32[1,4,128,4,128]{4,3,2,1,0:T(4,128)} %copy-done.13) | copy-start | bytes 3145732
  269.1 5.8 copy-start.10
  269.1 5.8 copy-start.23
  274.9 5.8 copy-start.3
  274.9 5.8 copy-start.4
  274.9 5.8 copy-start.5
  274.9 5.8 copy-start.6
  387.5 39.6 %all-to-all-start.14 = ((f32[2,4,512,128]{3,1,0,2:T(4,128)}), f32[2,4,512,128]{3,1,0,2:T(4,128)S(1)}, u32[]{:S(2)}, u32[]{:S(2)}) async-start(f32[2,4,512,128]{3,1,0,2:T(4,128)} %copy.152), calls=%async_computation.14 | async-start | bytes 4194304 | tf_op jit(solution)/shard_map/all_to_all | solution.py:31
  427.1 1.3 copy-start
  428.4 34.4 %all-to-all-start.12 = ((f32[2,4,512,128]{3,1,0,2:T(4,128)}), f32[2,4,512,128]{3,1,0,2:T(4,128)S(1)}, u32[]{:S(2)}, u32[]{:S(2)}) async-start(f32[2,4,512,128]{3,1,0,2:T(4,128)} %copy.148), calls=%async_computation.12 | async-start | bytes 4194304 | tf_op jit(solution)/shard_map/all_to_all | solution.py:31
  462.8 35.1 %all-to-all-start.8 = ((f32[2,4,512,128]{3,1,0,2:T(4,128)}), f32[2,4,512,128]{3,1,0,2:T(4,128)}, u32[]{:S(2)}, u32[]{:S(2)}) async-start(f32[2,4,512,128]{3,1,0,2:T(4,128)} %copy.137), calls=%async_computation.8 | async-start | bytes 4194304 | tf_op jit(solution)/shard_map/all_to_all | solution.py:31
  497.9 35.3 %all-to-all-start.4 = ((f32[2,4,512,128]{3,1,0,2:T(4,128)}), f32[2,4,512,128]{3,1,0,2:T(4,128)}, u32[]{:S(2)}, u32[]{:S(2)}) async-start(f32[2,4,512,128]{3,1,0,2:T(4,128)} %copy.126), calls=%async_computation.4 | async-start | bytes 4194304 | tf_op jit(solution)/shard_map/all_to_all | solution.py:31
  533.1 15.8 %all-to-all-start.9 = ((bf16[1,256,4,128]{3,2,0,1:T(4,128)(2,1)}), bf16[1,256,4,128]{3,2,0,1:T(4,128)(2,1)S(1)}, u32[]{:S(2)}, u32[]{:S(2)}) async-start(bf16[1,256,4,128]{3,2,0,1:T(4,128)(2,1)} %copy.139), calls=%async_computation.9 | async-start | bytes 524288 | tf_op jit(solution)/shard_map/all_to_all | solution.py:35
  548.9 23.2 %all-to-all-start.15 = ((f32[1,256,4,128]{3,2,0,1:T(4,128)}), f32[1,256,4,128]{3,2,0,1:T(4,128)S(1)}, u32[]{:S(2)}, u32[]{:S(2)}) async-start(f32[1,256,4,128]{3,2,0,1:T(4,128)} %copy.154), calls=%async_computation.15 | async-start | bytes 1048576 | tf_op jit(solution)/shard_map/all_to_all | solution.py:35
  572.1 20.9 %all-to-all-start.13 = ((f32[1,256,4,128]{3,2,0,1:T(4,128)}), f32[1,256,4,128]{3,2,0,1:T(4,128)S(1)}, u32[]{:S(2)}, u32[]{:S(2)}) async-start(f32[1,256,4,128]{3,2,0,1:T(4,128)} %copy.150), calls=%async_computation.13 | async-start | bytes 1048576 | tf_op jit(solution)/shard_map/all_to_all | solution.py:35
  586.8 12.6 %copy-start.8 = (bf16[1024,128]{1,0:T(8,128)(2,1)S(1)}, bf16[1024,128]{1,0:T(8,128)(2,1)}, u32[]{:S(2)}) copy-start(bf16[1024,128]{1,0:T(8,128)(2,1)} %param.10) | copy-start | bytes 786436
  593.0 18.2 %all-to-all-start.5 = ((f32[1,256,4,128]{3,2,0,1:T(4,128)}), f32[1,256,4,128]{3,2,0,1:T(4,128)S(1)}, u32[]{:S(2)}, u32[]{:S(2)}) async-start(f32[1,256,4,128]{3,2,0,1:T(4,128)} %copy.128), calls=%async_computation.5 | async-start | bytes 1048576 | tf_op jit(solution)/shard_map/all_to_all | solution.py:35
  598.4 12.9 %copy-start.22 = (bf16[1024,128]{1,0:T(8,128)(2,1)S(1)}, bf16[1024,128]{1,0:T(8,128)(2,1)}, u32[]{:S(2)}) copy-start(bf16[1024,128]{1,0:T(8,128)(2,1)} %param.7) | copy-start | bytes 786436
where the time goes:
time: 621 us; the launch traced here: 612 us
  matrix products  254 us (41%)
  waiting for transfers between devices  184 us (30%)
  starting transfers between devices  108 us (17%)
  local copies, waits for them, and re-layouts  51.6 us (8%)
  other arithmetic  12.8 us (2%)
    dot_general x32, matrix products, apply_second(): return jnp.einsum('rbc,bj->rjc', values, table, precision=HIGHEST)  201 us
    all_to_all x4, waiting for transfers between devices, inverse_columns(): lax.all_to_all(values, ('ctx', 'tp', 'dp'), split_axis=2, concat_axis=1,...  92.8 us
    all_to_all x4, waiting for transfers between devices, spectrum_rows(): lax.all_to_all(values, ('ctx', 'tp', 'dp'), split_axis=1, concat_axis=2,...  50.5 us
    all_to_all x4, starting transfers between devices, spectrum_rows(): lax.all_to_all(values, ('ctx', 'tp', 'dp'), split_axis=1, concat_axis=2,...  27.9 us
    all_to_all x4, starting transfers between devices, spread_input(): lax.all_to_all(values, ('ctx', 'tp', 'dp'), split_axis=2, concat_axis=1,...  27.2 us
    all_to_all x4, starting transfers between devices, output_rows(): lax.all_to_all(values, ('ctx', 'tp', 'dp'), split_axis=1, concat_axis=2,...  26.4 us
    all_to_all x4, starting transfers between devices, inverse_columns(): lax.all_to_all(values, ('ctx', 'tp', 'dp'), split_axis=2, concat_axis=1,...  26.3 us
    all_to_all x4, waiting for transfers between devices, output_rows(): lax.all_to_all(values, ('ctx', 'tp', 'dp'), split_axis=1, concat_axis=2,...  20.8 us
  transfers between devices with their start and end apart: 16, of which 15 were waited for; matrix products, arithmetic and copies ran while one was open for 28% of the time, Pallas kernels for 0%

commit v1 on v0

v1 whole, which is shorter than its diff:
```python
import functools
import math

import jax
import jax.numpy as jnp
import ml_dtypes
import numpy as np
from jax import lax
from jax.experimental import pallas as pl
from jax.experimental.pallas import tpu as pltpu
from jax.sharding import PartitionSpec as P

AXES = ("ctx", "tp", "dp")
SEQ = 131072
ROWS = 8
LANES = 128
FIRST = 1024
SECOND = 128
HALF = FIRST // 2
QUARTER = FIRST // 4
CHUNK = 64
STEPS = QUARTER // CHUNK
BLOCK = 4 * CHUNK
ARRAYS = 4
PIECE = ARRAYS * ROWS
PAIR = 2 * ROWS
STRIDE = ROWS + 1
BACK = FIRST
FORWARD_SECOND = BACK + FIRST
INVERSE_SECOND = FORWARD_SECOND + 2 * SECOND
TABLE_WIDTH = INVERSE_SECOND + 2 * SECOND
SECOND_SCALE = 1.66569
BF16 = jnp.bfloat16
F32 = jnp.float32


@functools.cache
def make_tables():
    quarter = QUARTER * np.arange(4).reshape(1, 4, 1)
    first = (np.arange(QUARTER).reshape(STEPS, 1, CHUNK) + quarter).reshape(FIRST)
    position, second = np.arange(FIRST), np.arange(SECOND)
    product = (4 * first[:, None] + 1) * (2 * position[None, :] + 1) % (8 * FIRST)
    first_phase = 2 * np.pi * product / (8 * FIRST)
    twist_phase = 2 * np.pi * (4 * first[:, None] + 1) * (second[None, :] - SECOND // 2) / (4 * SEQ)
    forward_phase = twist_phase + np.pi / 4 * (first // QUARTER)[:, None]
    second_phase = 2 * np.pi * ((second[:, None] * second[None, :]) % SECOND) / SECOND
    scale = (SEQ * math.sqrt(SEQ) * SECOND_SCALE**3 * math.sqrt(2.0)) ** (-1 / 3)
    back = [np.cos(twist_phase) + np.sin(twist_phase), np.cos(twist_phase) - np.sin(twist_phase)]
    twist = scale * np.concatenate([np.cos(forward_phase), np.sin(forward_phase)] + back, axis=1)
    cos_second, sin_second = np.cos(second_phase), np.sin(second_phase)
    forward_second = np.block([[cos_second, sin_second], [-sin_second, cos_second]])
    inverse_second = np.block([[cos_second, -sin_second], [sin_second, cos_second]])

    columns = position.reshape(QUARTER, 4).T.reshape(FIRST)
    lowest = first_phase.reshape(STEPS // 2, 2, 4, CHUNK, FIRST)[:, :, 0].reshape(STEPS // 2, 2 * CHUNK, FIRST)
    lowest = lowest[:, :, columns]
    joined = np.zeros((FIRST, TABLE_WIDTH), ml_dtypes.bfloat16)
    joined[:HALF, :FIRST] = np.concatenate([np.cos(lowest), np.sin(lowest)], axis=1).reshape(HALF, FIRST)
    half_phase = first_phase[:, :HALF].T
    joined[:HALF, BACK : BACK + FIRST] = np.cos(half_phase - np.pi / 4)
    joined[HALF:, BACK : BACK + FIRST] = np.cos(half_phase + np.pi / 4)
    for column, table in ((FORWARD_SECOND, forward_second), (INVERSE_SECOND, inverse_second)):
        table = SECOND_SCALE * np.concatenate([table, table], axis=0)
        joined[: 4 * SECOND, column : column + 2 * SECOND] = table
    return joined, twist.astype(np.float32)


def pack_kernel(filter_hbm, first_hbm, second_hbm, gate_hbm, upstream_hbm, out_ref, local, scratch, sems):
    sources = (filter_hbm, first_hbm, second_hbm, gate_hbm, upstream_hbm)
    copies = [
        pltpu.make_async_copy(source, local.at[index], sems.at[index])
        for index, source in enumerate(sources)
    ]
    for copy in copies:
        copy.start()
    for index in range(ARRAYS):
        copies[index].wait()
        if index == ARRAYS - 1:
            copies[ARRAYS].wait()
        for row in range(ROWS):
            span = pl.ds(row * LANES, LANES)
            block = local[index, span, :]
            if index == ARRAYS - 1:
                block = (block.astype(F32) * local[ARRAYS, span, :].astype(F32)).astype(BF16)
            scratch[index, pl.ds(row, LANES, stride=STRIDE), :] = block.T.astype(F32)
        if index % 2:
            for channel in range(LANES):
                rows = pl.ds(channel * STRIDE, ROWS)
                pair = jnp.concatenate([scratch[index - 1, rows, :], scratch[index, rows, :]], axis=0)
                out_ref[channel, index // 2 * PAIR : (index // 2 + 1) * PAIR, :] = pair.astype(BF16)


def unpack_kernel(
    in_ref, gate_ref, upstream_ref, mixed_hbm, signal_hbm, gate_out_hbm, filter_hbm,
    scratch, halves, filter_out, sems,
):
    mirrored = lax.axis_index("ctx") >= lax.axis_size("ctx") // 2
    targets = (mixed_hbm, gate_out_hbm, signal_hbm, filter_hbm)
    copies = []
    for index in (3, 2, 0, 1):
        if index in (3, 0):
            for channel in range(LANES):
                pair = in_ref[channel, index // 2 * PAIR : (index // 2 + 1) * PAIR, :].astype(F32)
                rows = pl.ds(channel * STRIDE, ROWS)
                scratch[index // 2 * 2, rows, :] = pair[:ROWS]
                scratch[index // 2 * 2 + 1, rows, :] = pair[ROWS:]
        for row in range(ROWS):
            place = jnp.where(mirrored, ROWS - 1 - row, row)
            span = pl.ds(pl.multiple_of(place * LANES, LANES), LANES)
            block = scratch[index, pl.ds(row, LANES, stride=STRIDE), :]
            block = block.astype(BF16).T.astype(F32)
            if index == 0:
                halves[index, span, :] = (gate_ref[span, :].astype(F32) * block).astype(BF16)
            elif index == 1:
                halves[index, span, :] = (upstream_ref[span, :].astype(F32) * block).astype(BF16)
            elif index == 2:
                halves[index, span, :] = block.astype(BF16)
            else:
                filter_out[span, :] = block
        source = filter_out if index == 3 else halves.at[index]
        copies.append(pltpu.make_async_copy(source, targets[index], sems.at[index]))
        copies[-1].start()
    for copy in copies:
        copy.wait()


def two_pass(real, imag, table_ref, column):
    real_high, imag_high = real.astype(BF16), imag.astype(BF16)
    real_low = (real - real_high.astype(F32)).astype(BF16)
    imag_low = (imag - imag_high.astype(F32)).astype(BF16)
    joined = jnp.concatenate([real_high, imag_high, real_low, imag_low], axis=1)
    table = table_ref[: 4 * SECOND, column : column + 2 * SECOND]
    out = jnp.dot(joined, table, preferred_element_type=F32)
    return out[:, :SECOND], out[:, SECOND:]


def convolve_kernel(in_ref, table_ref, twist_ref, out_ref, rows_ref, values_ref, sum_ref, difference_ref):
    lanes = [slice(index * LANES, (index + 1) * LANES) for index in range(ARRAYS)]
    pairs = [slice(start, start + 2 * LANES) for start in range(0, ARRAYS * LANES, 2 * LANES)]

    def lay_out(pair):
        arrived = in_ref[:, pair * PAIR : (pair + 1) * PAIR, :].astype(F32)
        for index in range(2):
            part = lanes[2 * pair + index]
            rows_ref[2 * pair + index] = arrived[:, index * ROWS : (index + 1) * ROWS, :].reshape(FIRST, LANES)
            for residue in range(4):
                values_ref[residue * QUARTER : (residue + 1) * QUARTER, part] = (
                    rows_ref[2 * pair + index, pl.ds(residue, QUARTER, stride=4), :].astype(BF16)
                )

    def rows_of(step):
        return slice(step * BLOCK, (step + 1) * BLOCK)

    def first_factor(double, pair):
        rows = rows_of(double)
        p0, p1, p2, p3 = (
            jnp.dot(
                table_ref[rows, residue * QUARTER : (residue + 1) * QUARTER],
                values_ref[residue * QUARTER : (residue + 1) * QUARTER, pairs[pair]],
                preferred_element_type=F32,
            )
            for residue in range(4)
        )
        s02, d02, s13, d13 = p0 + p2, p0 - p2, p1 + p3, p1 - p3
        real, imag = slice(0, 2 * CHUNK), slice(2 * CHUNK, 4 * CHUNK)
        reals = [s02[real] + s13[real], d02[real] - d13[imag], s02[real] - s13[real], d02[real] + d13[imag]]
        imags = [s02[imag] + s13[imag], d02[imag] + d13[real], s02[imag] - s13[imag], d02[imag] - d13[real]]
        return [
            tuple(
                jnp.concatenate([value[step * CHUNK : (step + 1) * CHUNK] for value in values], axis=0)
                for values in (reals, imags)
            )
            for step in range(2)
        ]

    def second_factor(step, turned):
        real, imag = (jnp.concatenate(parts, axis=1) for parts in zip(*turned))
        cos_twist, sin_twist = twist_ref[rows_of(step), :SECOND], twist_ref[rows_of(step), SECOND : 2 * SECOND]
        return [
            two_pass(
                real[:, part] * cos_twist - imag[:, part] * sin_twist,
                real[:, part] * sin_twist + imag[:, part] * cos_twist,
                table_ref,
                FORWARD_SECOND,
            )
            for part in lanes
        ]

    def multiply(spectra):
        (fr, fi), (ar, ai), (br, bi), (mr, mi) = spectra
        products = [
            (fr * ar - fi * ai, fr * ai + fi * ar),
            (fr * br - fi * bi, fr * bi + fi * br),
            (fr * mr + fi * mi, fr * mi - fi * mr),
            (mr * br + mi * bi, mi * br - mr * bi),
        ]
        return [two_pass(real, imag, table_ref, INVERSE_SECOND) for real, imag in products]

    def store(step, results):
        sum_twist = twist_ref[rows_of(step), 2 * SECOND : 3 * SECOND]
        difference_twist = twist_ref[rows_of(step), 3 * SECOND :]
        for part, (real, imag) in zip(lanes, results):
            sum_ref[rows_of(step), part] = (real * difference_twist + imag * sum_twist).astype(BF16)
            difference_ref[rows_of(step), part] = (real * sum_twist - imag * difference_twist).astype(BF16)

    step = HALF // 4
    count = step // ROWS
    early = rows_of(STEPS - 3).stop

    def way_back(part, rows):
        columns = slice(BACK + rows.start, BACK + rows.stop)
        even = jnp.dot(
            table_ref[part * step : (part + 1) * step, columns], sum_ref[rows, :], preferred_element_type=F32
        )
        odd = jnp.dot(
            table_ref[HALF + part * step : HALF + (part + 1) * step, columns],
            difference_ref[rows, :],
            preferred_element_type=F32,
        )
        return even, odd

    turned, spectra, results, partial = {}, {}, {}, {}

    def begin(double, pair):
        for index, value in enumerate(first_factor(double, pair)):
            turned.setdefault(2 * double + index, []).append(value)

    for pair in range(2):
        lay_out(pair)
        begin(0, pair)
    for turn in range(1, STEPS + 3):
        if turn % 2 and turn + 1 < STEPS:
            for pair in range(2):
                begin((turn + 1) // 2, pair)
        if 0 <= turn - 1 < STEPS:
            spectra[turn - 1] = second_factor(turn - 1, turned.pop(turn - 1))
        if turn > STEPS:
            for part in range(2 * (turn - STEPS - 1), 2 * (turn - STEPS)):
                partial[part] = way_back(part, slice(0, early))
        if 0 <= turn - 2 < STEPS:
            results[turn - 2] = multiply(spectra.pop(turn - 2))
        if 0 <= turn - 3 < STEPS:
            store(turn - 3, results.pop(turn - 3))

    for part in range(HALF // step):
        even, odd = way_back(part, slice(early, FIRST))
        even, odd = even + partial[part][0], odd + partial[part][1]
        for result, places in (
            (even + odd, range(part * count, (part + 1) * count)),
            (even - odd, range(LANES - 1 - part * count, LANES - 1 - (part + 1) * count, -1)),
        ):
            pieces = [result[:, lane].reshape(count, ROWS, LANES) for lane in lanes]
            joined = jnp.concatenate(pieces, axis=1).astype(BF16)
            for index, place in enumerate(places):
                out_ref[place] = joined[index]


def vmem():
    return pl.BlockSpec(memory_space=pltpu.VMEM)


def hbm():
    return pl.BlockSpec(memory_space=pltpu.HBM)


def exchange(pieces):
    return lax.all_to_all(pieces, AXES, split_axis=0, concat_axis=0, tiled=True)


def on_device(signal_first, gate_first, signal_second, gate_second, upstream_second, filter_param):
    positions = ROWS * LANES
    local = jax.ShapeDtypeStruct((positions, LANES), BF16)
    pieces = jax.ShapeDtypeStruct((LANES, PIECE, LANES), BF16)
    sources = (filter_param, signal_first, signal_second, gate_second, upstream_second)
    packed = pl.pallas_call(
        pack_kernel,
        out_shape=pieces,
        in_specs=[hbm()] * 5,
        out_specs=vmem(),
        scratch_shapes=[
            pltpu.VMEM((5, positions, LANES), BF16),
            pltpu.VMEM((ARRAYS, STRIDE * LANES, LANES), F32),
            pltpu.SemaphoreType.DMA((5,)),
        ],
        compiler_params=pltpu.CompilerParams(vmem_limit_bytes=40 * 1024 * 1024),
        cost_estimate=pl.CostEstimate(flops=20_000_000_000, bytes_accessed=2_400_000, transcendentals=0),
        name="pack",
    )(*[pltpu.with_memory_space_constraint(value, pltpu.HBM) for value in sources])
    convolved = pl.pallas_call(
        convolve_kernel,
        out_shape=pieces,
        in_specs=[vmem()] * 3,
        out_specs=vmem(),
        scratch_shapes=[pltpu.VMEM((ARRAYS, FIRST, LANES), F32)]
        + [pltpu.VMEM((FIRST, ARRAYS * LANES), BF16)] * 3,
        compiler_params=pltpu.CompilerParams(vmem_limit_bytes=40 * 1024 * 1024),
        name="convolve",
    )(exchange(packed), *make_tables())
    return pl.pallas_call(
        unpack_kernel,
        out_shape=(local, local, local, jax.ShapeDtypeStruct((positions, LANES), F32)),
        in_specs=[vmem()] * 3,
        out_specs=(hbm(),) * 4,
        scratch_shapes=[
            pltpu.VMEM((ARRAYS, STRIDE * LANES, LANES), F32),
            pltpu.VMEM((3, positions, LANES), BF16),
            pltpu.VMEM((positions, LANES), F32),
            pltpu.SemaphoreType.DMA((ARRAYS,)),
        ],
        compiler_params=pltpu.CompilerParams(vmem_limit_bytes=40 * 1024 * 1024),
        name="unpack",
    )(exchange(convolved), gate_first, upstream_second)


def solution(mesh):
    spec = P(AXES, None)
    return jax.shard_map(
        on_device,
        mesh=mesh,
        in_specs=(spec,) * 6,
        out_specs=(spec,) * 4,
        check_vma=False,
    )
```

time: 621 us -> 61.8 us (0.10); the launches traced: 612 us -> 61.7 us
  matrix products: 254 us -> 0 us
  waiting for transfers between devices: 184 us -> 0 us
  starting transfers between devices: 108 us -> 0 us
  blocking collectives: 0 us -> 53 us
  local copies, waits for them, and re-layouts: 51.6 us -> 0.02 us
  other arithmetic: 12.8 us -> 0 us
  Pallas kernels: 0 us -> 7.98 us
    dot_general x48 -> x0, matrix products: 254 us -> none  [the longest x32 201 us: apply_second(): return jnp.einsum('rbc,bj->rjc', values, table, precision=HIGHEST)]
    all_to_all x16 -> x0, waiting for transfers between devices: 184 us -> none  [the longest x4 92.8 us: inverse_columns(): lax.all_to_all(values, ('ctx', 'tp', 'dp'), split_axis=2, concat_axis=1,...]
    all_to_all x16 -> x0, starting transfers between devices: 108 us -> none  [the longest x4 27.9 us: spectrum_rows(): lax.all_to_all(values, ('ctx', 'tp', 'dp'), split_axis=1, concat_axis=2,...]
    all_to_all x0 -> x2, blocking collectives: none -> 53 us  [exchange(): return lax.all_to_all(pieces, AXES, split_axis=0, concat_axis=0, tiled=True)]
    another operation x8 -> x0, local copies, waits for them, and re-layouts: 21.5 us -> none  [the longest x4 10.8 us: inverse(): jnp.stack([back_real * cos_back - back_imag * sin_back, back_real * sin_b...]
    all_to_all x19 -> x0, local copies, waits for them, and re-layouts: 14.6 us -> none  [the longest x4 7.61 us: inverse_columns(): lax.all_to_all(values, ('ctx', 'tp', 'dp'), split_axis=2, concat_axis=1,...]
    another operation x8 -> x0, other arithmetic: 9.8 us -> none  [the longest x4 4.9 us: forward(): jnp.stack([cos_real * cos_fwd + imag_part * sin_fwd, imag_part * cos_fwd...]
    pallas_call x0 -> x3, Pallas kernels: none -> 7.98 us  [the longest x1 4.96 us: on_device(): pl.pallas_call(convolve_kernel, out_shape=pieces, in_specs=[vmem()] * 3,...]
  transfers between devices with their start and end apart: 16 -> 0, of which waited for: 15 -> 0; matrix products, arithmetic and copies ran while one was open for 28% -> 0% of each run, Pallas kernels for 0% -> 0%
where the time goes in v1:
time: 61.8 us; the launch traced here: 61.7 us
  blocking collectives  53 us (86%)
  Pallas kernels  7.98 us (13%)
  between operations  0.67 us (1%)
    all_to_all x2, blocking collectives, exchange(): return lax.all_to_all(pieces, AXES, split_axis=0, concat_axis=0, tiled=True)  53 us
    pallas_call x1, Pallas kernels, on_device(): pl.pallas_call(convolve_kernel, out_shape=pieces, in_specs=[vmem()] * 3,...  4.96 us
    pallas_call x1, Pallas kernels, on_device(): pl.pallas_call(pack_kernel, out_shape=pieces, in_specs=[hbm()] * 5, out_s...  1.73 us
    pallas_call x1, Pallas kernels, on_device(): pl.pallas_call(unpack_kernel, out_shape=(local, local, local, jax.ShapeDt...  1.29 us

profile of v1, /device:TPU:0, one launch (start us, length us, event | category | flops | bytes accessed | tf_op | source)
XLA Modules:
  0.0 61.7 jit_solution(8355657444491187271)
XLA Ops:
  0.6 0.0 copy-start.1
  0.6 0.0 copy-start
  0.7 1.7 %pack.1 = bf16[128,32,128]{2,1,0:T(8,128)(2,1)S(1)} custom-call(bf16[1024,128]{1,0:T(8,128)(2,1)} %filter_hbm.1, bf16[1024,128]{1,0:T(8,128)(2,1)} %first_hbm.1, bf16[1024,128]{1,0:T(8,128)(2,1)} %second_hbm.1, bf16[1024,128]{1,0:T(8,128)(2,1)} %gate_hbm.1, bf16[1024,128]{1,0:T(8,128)(2,1)} %upstream_ref.1), custom_call_target="tpu_custom_call" | custom-call | flops 20000000000 | bytes 2400000 | tf_op jit(solution)/shard_map/pack/pallas_call | solution.py:275
  2.4 30.0 %all_to_all.10.in_ref = bf16[128,32,128]{2,1,0:T(8,128)(2,1)S(1)} all-to-all(bf16[128,32,128]{2,1,0:T(8,128)(2,1)S(1)} %pack.1), channel_id=1, replica_groups=mesh['ctx'=8,'tp'=8,'dp'=2] {'ctx','tp','dp'}, dimensions={0} | all-to-all | bytes 2097152 | tf_op jit(solution)/shard_map/all_to_all | solution.py:267
  32.4 0.0 copy-done.1
  32.4 0.0 copy-done
  32.4 0.0 copy-start.2
  32.4 0.0 copy-start.3
  32.4 5.0 %convolve.1 = bf16[128,32,128]{2,1,0:T(8,128)(2,1)S(1)} custom-call(bf16[128,32,128]{2,1,0:T(8,128)(2,1)S(1)} %all_to_all.10.in_ref, bf16[1024,2560]{1,0:T(8,128)(2,1)S(1)} %copy-done, f32[1024,512]{1,0:T(8,128)S(1)} %copy-done.1), custom_call_target="tpu_custom_call" | custom-call | tf_op jit(solution)/shard_map/convolve/pallas_call | solution.py:289
  37.4 23.0 %all_to_all.11.in_ref = bf16[128,32,128]{2,1,0:T(8,128)(2,1)S(1)} all-to-all(bf16[128,32,128]{2,1,0:T(8,128)(2,1)S(1)} %convolve.1), channel_id=1, replica_groups=mesh['ctx'=8,'tp'=8,'dp'=2] {'ctx','tp','dp'}, dimensions={0} | all-to-all | bytes 2097152 | tf_op jit(solution)/shard_map/all_to_all | solution.py:267
  60.4 0.0 copy-done.2
  60.4 0.0 copy-done.3
  60.4 1.3 %unpack.1 = (bf16[1024,128]{1,0:T(8,128)(2,1)}, bf16[1024,128]{1,0:T(8,128)(2,1)}, bf16[1024,128]{1,0:T(8,128)(2,1)}, f32[1024,128]{1,0:T(8,128)}) custom-call(bf16[128,32,128]{2,1,0:T(8,128)(2,1)S(1)} %all_to_all.11.in_ref, bf16[1024,128]{1,0:T(8,128)(2,1)S(1)} %copy-done.3, bf16[1024,128]{1,0:T(8,128)(2,1)S(1)} %copy-done.2), custom_call_target="tpu_custom_call" | custom-call | tf_op jit(solution)/shard_map/unpack/pallas_call | solution.py:299
Async XLA Ops:
  0.6 31.8 %copy-start.1 = (f32[1024,512]{1,0:T(8,128)S(1)}, f32[1024,512]{1,0:T(8,128)}, u32[]{:S(2)}) copy-start(f32[1024,512]{1,0:T(8,128)} %constant.5.clone.twist_ref) | copy-start | bytes 6291460
  0.6 31.8 %copy-start = (bf16[1024,2560]{1,0:T(8,128)(2,1)S(1)}, bf16[1024,2560]{1,0:T(8,128)(2,1)}, u32[]{:S(2)}) copy-start(bf16[1024,2560]{1,0:T(8,128)(2,1)} %constant.4.clone.table_ref) | copy-start | bytes 15728644
  32.4 28.0 %copy-start.2 = (bf16[1024,128]{1,0:T(8,128)(2,1)S(1)}, bf16[1024,128]{1,0:T(8,128)(2,1)}, u32[]{:S(2)}) copy-start(bf16[1024,128]{1,0:T(8,128)(2,1)} %upstream_ref.1) | copy-start | bytes 786436
  32.4 28.0 %copy-start.3 = (bf16[1024,128]{1,0:T(8,128)(2,1)S(1)}, bf16[1024,128]{1,0:T(8,128)(2,1)}, u32[]{:S(2)}) copy-start(bf16[1024,128]{1,0:T(8,128)(2,1)} %gate_ref.1) | copy-start | bytes 786436

commit v2 on v1

--- a/solution.py
+++ b/solution.py
@@ -74,9 +74,9 @@
     for copy in copies:
         copy.start()
     for index in range(ARRAYS):
-        copies[index].wait()
-        if index == ARRAYS - 1:
-            copies[ARRAYS].wait()
+        if index % 2 == 0:
+            for copy in copies[:2] if index == 0 else copies[2:]:
+                copy.wait()
         for row in range(ROWS):
             span = pl.ds(row * LANES, LANES)
             block = local[index, span, :]
@@ -119,7 +119,9 @@
                 filter_out[span, :] = block
         source = filter_out if index == 3 else halves.at[index]
         copies.append(pltpu.make_async_copy(source, targets[index], sems.at[index]))
-        copies[-1].start()
+        if index in (2, 1):
+            for copy in copies[-2:]:
+                copy.start()
     for copy in copies:
         copy.wait()
 
@@ -142,7 +144,7 @@
         arrived = in_ref[:, pair * PAIR : (pair + 1) * PAIR, :].astype(F32)
         for index in range(2):
             part = lanes[2 * pair + index]
-            rows_ref[2 * pair + index] = arrived[:, index * ROWS : (index + 1) * ROWS, :].reshape(FIRST, LANES)
+            rows_ref[2 * pair + index, :FIRST, :] = arrived[:, index * ROWS : (index + 1) * ROWS, :].reshape(FIRST, LANES)
             for residue in range(4):
                 values_ref[residue * QUARTER : (residue + 1) * QUARTER, part] = (
                     rows_ref[2 * pair + index, pl.ds(residue, QUARTER, stride=4), :].astype(BF16)
@@ -279,7 +281,7 @@
         out_specs=vmem(),
         scratch_shapes=[
             pltpu.VMEM((5, positions, LANES), BF16),
-            pltpu.VMEM((ARRAYS, STRIDE * LANES, LANES), F32),
+            pltpu.VMEM((ARRAYS, STRIDE * LANES + PAIR, LANES), F32),
             pltpu.SemaphoreType.DMA((5,)),
         ],
         compiler_params=pltpu.CompilerParams(vmem_limit_bytes=40 * 1024 * 1024),
@@ -291,7 +293,7 @@
         out_shape=pieces,
         in_specs=[vmem()] * 3,
         out_specs=vmem(),
-        scratch_shapes=[pltpu.VMEM((ARRAYS, FIRST, LANES), F32)]
+        scratch_shapes=[pltpu.VMEM((ARRAYS, FIRST + PAIR, LANES), F32)]
         + [pltpu.VMEM((FIRST, ARRAYS * LANES), BF16)] * 3,
         compiler_params=pltpu.CompilerParams(vmem_limit_bytes=40 * 1024 * 1024),
         name="convolve",
@@ -302,7 +304,7 @@
         in_specs=[vmem()] * 3,
         out_specs=(hbm(),) * 4,
         scratch_shapes=[
-            pltpu.VMEM((ARRAYS, STRIDE * LANES, LANES), F32),
+            pltpu.VMEM((ARRAYS, STRIDE * LANES + PAIR, LANES), F32),
             pltpu.VMEM((3, positions, LANES), BF16),
             pltpu.VMEM((positions, LANES), F32),
             pltpu.SemaphoreType.DMA((ARRAYS,)),

time: 61.8 us -> 61.8 us (level)
  no operation moved by 1% of the time
where the time goes in v2:
time: 61.8 us; the launch traced here: 61.7 us
  blocking collectives  53 us (86%)
  Pallas kernels  7.95 us (13%)
  between operations  0.67 us (1%)
    all_to_all x2, blocking collectives, exchange(): return lax.all_to_all(pieces, AXES, split_axis=0, concat_axis=0, tiled=True)  53 us
    pallas_call x1, Pallas kernels, on_device(): pl.pallas_call(convolve_kernel, out_shape=pieces, in_specs=[vmem()] * 3,...  4.96 us
    pallas_call x1, Pallas kernels, on_device(): pl.pallas_call(pack_kernel, out_shape=pieces, in_specs=[hbm()] * 5, out_s...  1.7 us
    pallas_call x1, Pallas kernels, on_device(): pl.pallas_call(unpack_kernel, out_shape=(local, local, local, jax.ShapeDt...  1.29 us

profile of v2, /device:TPU:0, one launch (start us, length us, event | category | flops | bytes accessed | tf_op | source)
XLA Modules:
  0.0 61.7 jit_solution(9861933871698022902)
XLA Ops:
  0.6 0.0 copy-start.1
  0.6 0.0 copy-start
  0.7 1.7 %pack.1 = bf16[128,32,128]{2,1,0:T(8,128)(2,1)S(1)} custom-call(bf16[1024,128]{1,0:T(8,128)(2,1)} %filter_hbm.1, bf16[1024,128]{1,0:T(8,128)(2,1)} %first_hbm.1, bf16[1024,128]{1,0:T(8,128)(2,1)} %second_hbm.1, bf16[1024,128]{1,0:T(8,128)(2,1)} %gate_hbm.1, bf16[1024,128]{1,0:T(8,128)(2,1)} %upstream_ref.1), custom_call_target="tpu_custom_call" | custom-call | flops 20000000000 | bytes 2400000 | tf_op jit(solution)/shard_map/pack/pallas_call | solution.py:277
  2.4 30.0 %all_to_all.10.in_ref = bf16[128,32,128]{2,1,0:T(8,128)(2,1)S(1)} all-to-all(bf16[128,32,128]{2,1,0:T(8,128)(2,1)S(1)} %pack.1), channel_id=1, replica_groups=mesh['ctx'=8,'tp'=8,'dp'=2] {'ctx','tp','dp'}, dimensions={0} | all-to-all | bytes 2097152 | tf_op jit(solution)/shard_map/all_to_all | solution.py:269
  32.4 0.0 copy-done.1
  32.4 0.0 copy-done
  32.4 0.0 copy-start.2
  32.4 0.0 copy-start.3
  32.4 5.0 %convolve.1 = bf16[128,32,128]{2,1,0:T(8,128)(2,1)S(1)} custom-call(bf16[128,32,128]{2,1,0:T(8,128)(2,1)S(1)} %all_to_all.10.in_ref, bf16[1024,2560]{1,0:T(8,128)(2,1)S(1)} %copy-done, f32[1024,512]{1,0:T(8,128)S(1)} %copy-done.1), custom_call_target="tpu_custom_call" | custom-call | tf_op jit(solution)/shard_map/convolve/pallas_call | solution.py:291
  37.3 23.0 %all_to_all.11.in_ref = bf16[128,32,128]{2,1,0:T(8,128)(2,1)S(1)} all-to-all(bf16[128,32,128]{2,1,0:T(8,128)(2,1)S(1)} %convolve.1), channel_id=1, replica_groups=mesh['ctx'=8,'tp'=8,'dp'=2] {'ctx','tp','dp'}, dimensions={0} | all-to-all | bytes 2097152 | tf_op jit(solution)/shard_map/all_to_all | solution.py:269
  60.4 0.0 copy-done.2
  60.4 0.0 copy-done.3
  60.4 1.3 %unpack.1 = (bf16[1024,128]{1,0:T(8,128)(2,1)}, bf16[1024,128]{1,0:T(8,128)(2,1)}, bf16[1024,128]{1,0:T(8,128)(2,1)}, f32[1024,128]{1,0:T(8,128)}) custom-call(bf16[128,32,128]{2,1,0:T(8,128)(2,1)S(1)} %all_to_all.11.in_ref, bf16[1024,128]{1,0:T(8,128)(2,1)S(1)} %copy-done.3, bf16[1024,128]{1,0:T(8,128)(2,1)S(1)} %copy-done.2), custom_call_target="tpu_custom_call" | custom-call | tf_op jit(solution)/shard_map/unpack/pallas_call | solution.py:301
Async XLA Ops:
  0.6 31.7 %copy-start.1 = (f32[1024,512]{1,0:T(8,128)S(1)}, f32[1024,512]{1,0:T(8,128)}, u32[]{:S(2)}) copy-start(f32[1024,512]{1,0:T(8,128)} %constant.5.clone.twist_ref) | copy-start | bytes 6291460
  0.6 31.7 %copy-start = (bf16[1024,2560]{1,0:T(8,128)(2,1)S(1)}, bf16[1024,2560]{1,0:T(8,128)(2,1)}, u32[]{:S(2)}) copy-start(bf16[1024,2560]{1,0:T(8,128)(2,1)} %constant.4.clone.table_ref) | copy-start | bytes 15728644
  32.4 28.0 %copy-start.2 = (bf16[1024,128]{1,0:T(8,128)(2,1)S(1)}, bf16[1024,128]{1,0:T(8,128)(2,1)}, u32[]{:S(2)}) copy-start(bf16[1024,128]{1,0:T(8,128)(2,1)} %upstream_ref.1) | copy-start | bytes 786436
  32.4 28.0 %copy-start.3 = (bf16[1024,128]{1,0:T(8,128)(2,1)S(1)}, bf16[1024,128]{1,0:T(8,128)(2,1)}, u32[]{:S(2)}) copy-start(bf16[1024,128]{1,0:T(8,128)(2,1)} %gate_ref.1) | copy-start | bytes 786436

commit v3 on v2

--- a/solution.py
+++ b/solution.py
@@ -207,7 +207,7 @@
 
     step = HALF // 4
     count = step // ROWS
-    early = rows_of(STEPS - 3).stop
+    early = rows_of(STEPS - 2).stop
 
     def way_back(part, rows):
         columns = slice(BACK + rows.start, BACK + rows.stop)
@@ -231,18 +231,18 @@
         lay_out(pair)
         begin(0, pair)
     for turn in range(1, STEPS + 3):
-        if turn % 2 and turn + 1 < STEPS:
-            for pair in range(2):
-                begin((turn + 1) // 2, pair)
-        if 0 <= turn - 1 < STEPS:
-            spectra[turn - 1] = second_factor(turn - 1, turned.pop(turn - 1))
+        if 0 <= turn - 3 < STEPS:
+            store(turn - 3, results.pop(turn - 3))
         if turn > STEPS:
             for part in range(2 * (turn - STEPS - 1), 2 * (turn - STEPS)):
                 partial[part] = way_back(part, slice(0, early))
         if 0 <= turn - 2 < STEPS:
             results[turn - 2] = multiply(spectra.pop(turn - 2))
-        if 0 <= turn - 3 < STEPS:
-            store(turn - 3, results.pop(turn - 3))
+        if 0 <= turn - 1 < STEPS:
+            spectra[turn - 1] = second_factor(turn - 1, turned.pop(turn - 1))
+        if turn % 2 and turn + 1 < STEPS:
+            for pair in range(2):
+                begin((turn + 1) // 2, pair)
 
     for part in range(HALF // step):
         even, odd = way_back(part, slice(early, FIRST))

time: 61.8 us -> 61.7 us (level)
  no operation moved by 1% of the time
where the time goes in v3:
time: 61.7 us; the launch traced here: 61.6 us
  blocking collectives  53 us (86%)
  Pallas kernels  7.86 us (13%)
  between operations  0.67 us (1%)
    all_to_all x2, blocking collectives, exchange(): return lax.all_to_all(pieces, AXES, split_axis=0, concat_axis=0, tiled=True)  53 us
    pallas_call x1, Pallas kernels, on_device(): pl.pallas_call(convolve_kernel, out_shape=pieces, in_specs=[vmem()] * 3,...  4.87 us
    pallas_call x1, Pallas kernels, on_device(): pl.pallas_call(pack_kernel, out_shape=pieces, in_specs=[hbm()] * 5, out_s...  1.7 us
    pallas_call x1, Pallas kernels, on_device(): pl.pallas_call(unpack_kernel, out_shape=(local, local, local, jax.ShapeDt...  1.29 us

profile of v3, /device:TPU:0, one launch (start us, length us, event | category | flops | bytes accessed | tf_op | source)
XLA Modules:
  0.0 61.6 jit_solution(5864034835516479545)
XLA Ops:
  0.6 0.0 copy-start.1
  0.6 0.0 copy-start
  0.7 1.7 %pack.1 = bf16[128,32,128]{2,1,0:T(8,128)(2,1)S(1)} custom-call(bf16[1024,128]{1,0:T(8,128)(2,1)} %filter_hbm.1, bf16[1024,128]{1,0:T(8,128)(2,1)} %first_hbm.1, bf16[1024,128]{1,0:T(8,128)(2,1)} %second_hbm.1, bf16[1024,128]{1,0:T(8,128)(2,1)} %gate_hbm.1, bf16[1024,128]{1,0:T(8,128)(2,1)} %upstream_ref.1), custom_call_target="tpu_custom_call" | custom-call | flops 20000000000 | bytes 2400000 | tf_op jit(solution)/shard_map/pack/pallas_call | solution.py:277
  2.4 30.0 %all_to_all.10.in_ref = bf16[128,32,128]{2,1,0:T(8,128)(2,1)S(1)} all-to-all(bf16[128,32,128]{2,1,0:T(8,128)(2,1)S(1)} %pack.1), channel_id=1, replica_groups=mesh['ctx'=8,'tp'=8,'dp'=2] {'ctx','tp','dp'}, dimensions={0} | all-to-all | bytes 2097152 | tf_op jit(solution)/shard_map/all_to_all | solution.py:269
  32.4 0.0 copy-done.1
  32.4 0.0 copy-done
  32.4 0.0 copy-start.2
  32.4 0.0 copy-start.3
  32.4 4.9 %convolve.1 = bf16[128,32,128]{2,1,0:T(8,128)(2,1)S(1)} custom-call(bf16[128,32,128]{2,1,0:T(8,128)(2,1)S(1)} %all_to_all.10.in_ref, bf16[1024,2560]{1,0:T(8,128)(2,1)S(1)} %copy-done, f32[1024,512]{1,0:T(8,128)S(1)} %copy-done.1), custom_call_target="tpu_custom_call" | custom-call | tf_op jit(solution)/shard_map/convolve/pallas_call | solution.py:291
  37.3 23.0 %all_to_all.11.in_ref = bf16[128,32,128]{2,1,0:T(8,128)(2,1)S(1)} all-to-all(bf16[128,32,128]{2,1,0:T(8,128)(2,1)S(1)} %convolve.1), channel_id=1, replica_groups=mesh['ctx'=8,'tp'=8,'dp'=2] {'ctx','tp','dp'}, dimensions={0} | all-to-all | bytes 2097152 | tf_op jit(solution)/shard_map/all_to_all | solution.py:269
  60.3 0.0 copy-done.2
  60.3 0.0 copy-done.3
  60.3 1.3 %unpack.1 = (bf16[1024,128]{1,0:T(8,128)(2,1)}, bf16[1024,128]{1,0:T(8,128)(2,1)}, bf16[1024,128]{1,0:T(8,128)(2,1)}, f32[1024,128]{1,0:T(8,128)}) custom-call(bf16[128,32,128]{2,1,0:T(8,128)(2,1)S(1)} %all_to_all.11.in_ref, bf16[1024,128]{1,0:T(8,128)(2,1)S(1)} %copy-done.3, bf16[1024,128]{1,0:T(8,128)(2,1)S(1)} %copy-done.2), custom_call_target="tpu_custom_call" | custom-call | tf_op jit(solution)/shard_map/unpack/pallas_call | solution.py:301
Async XLA Ops:
  0.6 31.7 %copy-start.1 = (f32[1024,512]{1,0:T(8,128)S(1)}, f32[1024,512]{1,0:T(8,128)}, u32[]{:S(2)}) copy-start(f32[1024,512]{1,0:T(8,128)} %constant.5.clone.twist_ref) | copy-start | bytes 6291460
  0.6 31.7 %copy-start = (bf16[1024,2560]{1,0:T(8,128)(2,1)S(1)}, bf16[1024,2560]{1,0:T(8,128)(2,1)}, u32[]{:S(2)}) copy-start(bf16[1024,2560]{1,0:T(8,128)(2,1)} %constant.4.clone.table_ref) | copy-start | bytes 15728644
  32.4 27.9 %copy-start.2 = (bf16[1024,128]{1,0:T(8,128)(2,1)S(1)}, bf16[1024,128]{1,0:T(8,128)(2,1)}, u32[]{:S(2)}) copy-start(bf16[1024,128]{1,0:T(8,128)(2,1)} %upstream_ref.1) | copy-start | bytes 786436
  32.4 27.9 %copy-start.3 = (bf16[1024,128]{1,0:T(8,128)(2,1)S(1)}, bf16[1024,128]{1,0:T(8,128)(2,1)}, u32[]{:S(2)}) copy-start(bf16[1024,128]{1,0:T(8,128)(2,1)} %gate_ref.1) | copy-start | bytes 786436

commit v4 on v3

--- a/solution.py
+++ b/solution.py
@@ -175,28 +175,28 @@
             for step in range(2)
         ]
 
-    def second_factor(step, turned):
-        real, imag = (jnp.concatenate(parts, axis=1) for parts in zip(*turned))
+    def second_factor(step, turned, index):
+        real, imag = turned[index // 2]
+        part = lanes[index % 2]
         cos_twist, sin_twist = twist_ref[rows_of(step), :SECOND], twist_ref[rows_of(step), SECOND : 2 * SECOND]
-        return [
-            two_pass(
-                real[:, part] * cos_twist - imag[:, part] * sin_twist,
-                real[:, part] * sin_twist + imag[:, part] * cos_twist,
-                table_ref,
-                FORWARD_SECOND,
-            )
-            for part in lanes
-        ]
-
-    def multiply(spectra):
+        return two_pass(
+            real[:, part] * cos_twist - imag[:, part] * sin_twist,
+            real[:, part] * sin_twist + imag[:, part] * cos_twist,
+            table_ref,
+            FORWARD_SECOND,
+        )
+
+    def multiply(spectra, index):
         (fr, fi), (ar, ai), (br, bi), (mr, mi) = spectra
-        products = [
-            (fr * ar - fi * ai, fr * ai + fi * ar),
-            (fr * br - fi * bi, fr * bi + fi * br),
-            (fr * mr + fi * mi, fr * mi - fi * mr),
-            (mr * br + mi * bi, mi * br - mr * bi),
-        ]
-        return [two_pass(real, imag, table_ref, INVERSE_SECOND) for real, imag in products]
+        if index == 0:
+            real, imag = fr * ar - fi * ai, fr * ai + fi * ar
+        elif index == 1:
+            real, imag = fr * br - fi * bi, fr * bi + fi * br
+        elif index == 2:
+            real, imag = fr * mr + fi * mi, fr * mi - fi * mr
+        else:
+            real, imag = mr * br + mi * bi, mi * br - mr * bi
+        return two_pass(real, imag, table_ref, INVERSE_SECOND)
 
     def store(step, results):
         sum_twist = twist_ref[rows_of(step), 2 * SECOND : 3 * SECOND]
@@ -236,13 +236,13 @@
         if turn > STEPS:
             for part in range(2 * (turn - STEPS - 1), 2 * (turn - STEPS)):
                 partial[part] = way_back(part, slice(0, early))
-        if 0 <= turn - 2 < STEPS:
-            results[turn - 2] = multiply(spectra.pop(turn - 2))
-        if 0 <= turn - 1 < STEPS:
-            spectra[turn - 1] = second_factor(turn - 1, turned.pop(turn - 1))
-        if turn % 2 and turn + 1 < STEPS:
-            for pair in range(2):
-                begin((turn + 1) // 2, pair)
+        for index in range(ARRAYS):
+            if 0 <= turn - 2 < STEPS:
+                results.setdefault(turn - 2, []).append(multiply(spectra[turn - 2], index))
+            if 0 <= turn - 1 < STEPS:
+                spectra.setdefault(turn - 1, []).append(second_factor(turn - 1, turned[turn - 1], index))
+            if turn % 2 and turn + 1 < STEPS and index % 2:
+                begin((turn + 1) // 2, index // 2)
 
     for part in range(HALF // step):
         even, odd = way_back(part, slice(early, FIRST))

time: 61.7 us -> 61.9 us (level)
  no operation moved by 1% of the time
where the time goes in v4:
time: 61.9 us; the launch traced here: 61.7 us
  blocking collectives  53 us (86%)
  Pallas kernels  8 us (13%)
  between operations  0.67 us (1%)
    all_to_all x2, blocking collectives, exchange(): return lax.all_to_all(pieces, AXES, split_axis=0, concat_axis=0, tiled=True)  53 us
    pallas_call x1, Pallas kernels, on_device(): pl.pallas_call(convolve_kernel, out_shape=pieces, in_specs=[vmem()] * 3,...  5.02 us
    pallas_call x1, Pallas kernels, on_device(): pl.pallas_call(pack_kernel, out_shape=pieces, in_specs=[hbm()] * 5, out_s...  1.7 us
    pallas_call x1, Pallas kernels, on_device(): pl.pallas_call(unpack_kernel, out_shape=(local, local, local, jax.ShapeDt...  1.29 us

profile of v4, /device:TPU:0, one launch (start us, length us, event | category | flops | bytes accessed | tf_op | source)
XLA Modules:
  0.0 61.7 jit_solution(17909857630421439416)
XLA Ops:
  0.6 0.0 copy-start.1
  0.6 0.0 copy-start
  0.7 1.7 %pack.1 = bf16[128,32,128]{2,1,0:T(8,128)(2,1)S(1)} custom-call(bf16[1024,128]{1,0:T(8,128)(2,1)} %filter_hbm.1, bf16[1024,128]{1,0:T(8,128)(2,1)} %first_hbm.1, bf16[1024,128]{1,0:T(8,128)(2,1)} %second_hbm.1, bf16[1024,128]{1,0:T(8,128)(2,1)} %gate_hbm.1, bf16[1024,128]{1,0:T(8,128)(2,1)} %upstream_ref.1), custom_call_target="tpu_custom_call" | custom-call | flops 20000000000 | bytes 2400000 | tf_op jit(solution)/shard_map/pack/pallas_call | solution.py:277
  2.4 30.0 %all_to_all.10.in_ref = bf16[128,32,128]{2,1,0:T(8,128)(2,1)S(1)} all-to-all(bf16[128,32,128]{2,1,0:T(8,128)(2,1)S(1)} %pack.1), channel_id=1, replica_groups=mesh['ctx'=8,'tp'=8,'dp'=2] {'ctx','tp','dp'}, dimensions={0} | all-to-all | bytes 2097152 | tf_op jit(solution)/shard_map/all_to_all | solution.py:269
  32.4 0.0 copy-done.1
  32.4 0.0 copy-done
  32.4 0.0 copy-start.2
  32.4 0.0 copy-start.3
  32.4 5.0 %convolve.1 = bf16[128,32,128]{2,1,0:T(8,128)(2,1)S(1)} custom-call(bf16[128,32,128]{2,1,0:T(8,128)(2,1)S(1)} %all_to_all.10.in_ref, bf16[1024,2560]{1,0:T(8,128)(2,1)S(1)} %copy-done, f32[1024,512]{1,0:T(8,128)S(1)} %copy-done.1), custom_call_target="tpu_custom_call" | custom-call | tf_op jit(solution)/shard_map/convolve/pallas_call | solution.py:291
  37.4 23.0 %all_to_all.11.in_ref = bf16[128,32,128]{2,1,0:T(8,128)(2,1)S(1)} all-to-all(bf16[128,32,128]{2,1,0:T(8,128)(2,1)S(1)} %convolve.1), channel_id=1, replica_groups=mesh['ctx'=8,'tp'=8,'dp'=2] {'ctx','tp','dp'}, dimensions={0} | all-to-all | bytes 2097152 | tf_op jit(solution)/shard_map/all_to_all | solution.py:269
  60.4 0.0 copy-done.2
  60.4 0.0 copy-done.3
  60.4 1.3 %unpack.1 = (bf16[1024,128]{1,0:T(8,128)(2,1)}, bf16[1024,128]{1,0:T(8,128)(2,1)}, bf16[1024,128]{1,0:T(8,128)(2,1)}, f32[1024,128]{1,0:T(8,128)}) custom-call(bf16[128,32,128]{2,1,0:T(8,128)(2,1)S(1)} %all_to_all.11.in_ref, bf16[1024,128]{1,0:T(8,128)(2,1)S(1)} %copy-done.3, bf16[1024,128]{1,0:T(8,128)(2,1)S(1)} %copy-done.2), custom_call_target="tpu_custom_call" | custom-call | tf_op jit(solution)/shard_map/unpack/pallas_call | solution.py:301
Async XLA Ops:
  0.6 31.7 %copy-start.1 = (f32[1024,512]{1,0:T(8,128)S(1)}, f32[1024,512]{1,0:T(8,128)}, u32[]{:S(2)}) copy-start(f32[1024,512]{1,0:T(8,128)} %constant.5.clone.twist_ref) | copy-start | bytes 6291460
  0.6 31.7 %copy-start = (bf16[1024,2560]{1,0:T(8,128)(2,1)S(1)}, bf16[1024,2560]{1,0:T(8,128)(2,1)}, u32[]{:S(2)}) copy-start(bf16[1024,2560]{1,0:T(8,128)(2,1)} %constant.4.clone.table_ref) | copy-start | bytes 15728644
  32.4 28.1 %copy-start.2 = (bf16[1024,128]{1,0:T(8,128)(2,1)S(1)}, bf16[1024,128]{1,0:T(8,128)(2,1)}, u32[]{:S(2)}) copy-start(bf16[1024,128]{1,0:T(8,128)(2,1)} %upstream_ref.1) | copy-start | bytes 786436
  32.4 28.1 %copy-start.3 = (bf16[1024,128]{1,0:T(8,128)(2,1)S(1)}, bf16[1024,128]{1,0:T(8,128)(2,1)}, u32[]{:S(2)}) copy-start(bf16[1024,128]{1,0:T(8,128)(2,1)} %gate_ref.1) | copy-start | bytes 786436

commit v5 on v3

--- a/solution.py
+++ b/solution.py
@@ -205,7 +205,7 @@
             sum_ref[rows_of(step), part] = (real * difference_twist + imag * sum_twist).astype(BF16)
             difference_ref[rows_of(step), part] = (real * sum_twist - imag * difference_twist).astype(BF16)
 
-    step = HALF // 4
+    step = HALF // 2
     count = step // ROWS
     early = rows_of(STEPS - 2).stop
 
@@ -234,8 +234,7 @@
         if 0 <= turn - 3 < STEPS:
             store(turn - 3, results.pop(turn - 3))
         if turn > STEPS:
-            for part in range(2 * (turn - STEPS - 1), 2 * (turn - STEPS)):
-                partial[part] = way_back(part, slice(0, early))
+            partial[turn - STEPS - 1] = way_back(turn - STEPS - 1, slice(0, early))
         if 0 <= turn - 2 < STEPS:
             results[turn - 2] = multiply(spectra.pop(turn - 2))
         if 0 <= turn - 1 < STEPS:

time: 61.7 us -> 61.7 us (level)
  no operation moved by 1% of the time
where the time goes in v5:
time: 61.7 us; the launch traced here: 61.6 us
  blocking collectives  53 us (86%)
  Pallas kernels  7.85 us (13%)
  between operations  0.67 us (1%)
    all_to_all x2, blocking collectives, exchange(): return lax.all_to_all(pieces, AXES, split_axis=0, concat_axis=0, tiled=True)  53 us
    pallas_call x1, Pallas kernels, on_device(): pl.pallas_call(convolve_kernel, out_shape=pieces, in_specs=[vmem()] * 3,...  4.87 us
    pallas_call x1, Pallas kernels, on_device(): pl.pallas_call(pack_kernel, out_shape=pieces, in_specs=[hbm()] * 5, out_s...  1.7 us
    pallas_call x1, Pallas kernels, on_device(): pl.pallas_call(unpack_kernel, out_shape=(local, local, local, jax.ShapeDt...  1.29 us

profile of v5, /device:TPU:0, one launch (start us, length us, event | category | flops | bytes accessed | tf_op | source)
XLA Modules:
  0.0 61.6 jit_solution(17014815479355671711)
XLA Ops:
  0.6 0.0 copy-start.1
  0.6 0.0 copy-start
  0.7 1.7 %pack.1 = bf16[128,32,128]{2,1,0:T(8,128)(2,1)S(1)} custom-call(bf16[1024,128]{1,0:T(8,128)(2,1)} %filter_hbm.1, bf16[1024,128]{1,0:T(8,128)(2,1)} %first_hbm.1, bf16[1024,128]{1,0:T(8,128)(2,1)} %second_hbm.1, bf16[1024,128]{1,0:T(8,128)(2,1)} %gate_hbm.1, bf16[1024,128]{1,0:T(8,128)(2,1)} %upstream_ref.1), custom_call_target="tpu_custom_call" | custom-call | flops 20000000000 | bytes 2400000 | tf_op jit(solution)/shard_map/pack/pallas_call | solution.py:276
  2.4 30.0 %all_to_all.10.in_ref = bf16[128,32,128]{2,1,0:T(8,128)(2,1)S(1)} all-to-all(bf16[128,32,128]{2,1,0:T(8,128)(2,1)S(1)} %pack.1), channel_id=1, replica_groups=mesh['ctx'=8,'tp'=8,'dp'=2] {'ctx','tp','dp'}, dimensions={0} | all-to-all | bytes 2097152 | tf_op jit(solution)/shard_map/all_to_all | solution.py:268
  32.4 0.0 copy-done.1
  32.4 0.0 copy-done
  32.4 0.0 copy-start.2
  32.4 0.0 copy-start.3
  32.4 4.9 %convolve.1 = bf16[128,32,128]{2,1,0:T(8,128)(2,1)S(1)} custom-call(bf16[128,32,128]{2,1,0:T(8,128)(2,1)S(1)} %all_to_all.10.in_ref, bf16[1024,2560]{1,0:T(8,128)(2,1)S(1)} %copy-done, f32[1024,512]{1,0:T(8,128)S(1)} %copy-done.1), custom_call_target="tpu_custom_call" | custom-call | tf_op jit(solution)/shard_map/convolve/pallas_call | solution.py:290
  37.2 23.0 %all_to_all.11.in_ref = bf16[128,32,128]{2,1,0:T(8,128)(2,1)S(1)} all-to-all(bf16[128,32,128]{2,1,0:T(8,128)(2,1)S(1)} %convolve.1), channel_id=1, replica_groups=mesh['ctx'=8,'tp'=8,'dp'=2] {'ctx','tp','dp'}, dimensions={0} | all-to-all | bytes 2097152 | tf_op jit(solution)/shard_map/all_to_all | solution.py:268
  60.3 0.0 copy-done.2
  60.3 0.0 copy-done.3
  60.3 1.3 %unpack.1 = (bf16[1024,128]{1,0:T(8,128)(2,1)}, bf16[1024,128]{1,0:T(8,128)(2,1)}, bf16[1024,128]{1,0:T(8,128)(2,1)}, f32[1024,128]{1,0:T(8,128)}) custom-call(bf16[128,32,128]{2,1,0:T(8,128)(2,1)S(1)} %all_to_all.11.in_ref, bf16[1024,128]{1,0:T(8,128)(2,1)S(1)} %copy-done.3, bf16[1024,128]{1,0:T(8,128)(2,1)S(1)} %copy-done.2), custom_call_target="tpu_custom_call" | custom-call | tf_op jit(solution)/shard_map/unpack/pallas_call | solution.py:300
Async XLA Ops:
  0.6 31.7 %copy-start.1 = (f32[1024,512]{1,0:T(8,128)S(1)}, f32[1024,512]{1,0:T(8,128)}, u32[]{:S(2)}) copy-start(f32[1024,512]{1,0:T(8,128)} %constant.5.clone.twist_ref) | copy-start | bytes 6291460
  0.6 31.7 %copy-start = (bf16[1024,2560]{1,0:T(8,128)(2,1)S(1)}, bf16[1024,2560]{1,0:T(8,128)(2,1)}, u32[]{:S(2)}) copy-start(bf16[1024,2560]{1,0:T(8,128)(2,1)} %constant.4.clone.table_ref) | copy-start | bytes 15728644
  32.4 27.9 %copy-start.2 = (bf16[1024,128]{1,0:T(8,128)(2,1)S(1)}, bf16[1024,128]{1,0:T(8,128)(2,1)}, u32[]{:S(2)}) copy-start(bf16[1024,128]{1,0:T(8,128)(2,1)} %upstream_ref.1) | copy-start | bytes 786436
  32.4 27.9 %copy-start.3 = (bf16[1024,128]{1,0:T(8,128)(2,1)S(1)}, bf16[1024,128]{1,0:T(8,128)(2,1)}, u32[]{:S(2)}) copy-start(bf16[1024,128]{1,0:T(8,128)(2,1)} %gate_ref.1) | copy-start | bytes 786436

commit v6 on v3

--- a/solution.py
+++ b/solution.py
@@ -230,19 +230,20 @@
     for pair in range(2):
         lay_out(pair)
         begin(0, pair)
-    for turn in range(1, STEPS + 3):
-        if 0 <= turn - 3 < STEPS:
+    for turn in range(1, STEPS + 1):
+        if turn >= 3:
             store(turn - 3, results.pop(turn - 3))
-        if turn > STEPS:
-            for part in range(2 * (turn - STEPS - 1), 2 * (turn - STEPS)):
-                partial[part] = way_back(part, slice(0, early))
-        if 0 <= turn - 2 < STEPS:
+        if turn >= 2:
             results[turn - 2] = multiply(spectra.pop(turn - 2))
-        if 0 <= turn - 1 < STEPS:
-            spectra[turn - 1] = second_factor(turn - 1, turned.pop(turn - 1))
+        spectra[turn - 1] = second_factor(turn - 1, turned.pop(turn - 1))
         if turn % 2 and turn + 1 < STEPS:
             for pair in range(2):
                 begin((turn + 1) // 2, pair)
+    results[STEPS - 1] = multiply(spectra.pop(STEPS - 1))
+    for last in (STEPS - 2, STEPS - 1):
+        store(last, results.pop(last))
+        for part in range(2 * (last - STEPS + 2), 2 * (last - STEPS + 3)):
+            partial[part] = way_back(part, slice(0, early))
 
     for part in range(HALF // step):
         even, odd = way_back(part, slice(early, FIRST))

time: 61.7 us -> 61.7 us (level)
  no operation moved by 1% of the time
where the time goes in v6:
time: 61.7 us; the launch traced here: 61.6 us
  blocking collectives  53 us (86%)
  Pallas kernels  7.87 us (13%)
  between operations  0.67 us (1%)
    all_to_all x2, blocking collectives, exchange(): return lax.all_to_all(pieces, AXES, split_axis=0, concat_axis=0, tiled=True)  53 us
    pallas_call x1, Pallas kernels, on_device(): pl.pallas_call(convolve_kernel, out_shape=pieces, in_specs=[vmem()] * 3,...  4.89 us
    pallas_call x1, Pallas kernels, on_device(): pl.pallas_call(pack_kernel, out_shape=pieces, in_specs=[hbm()] * 5, out_s...  1.7 us
    pallas_call x1, Pallas kernels, on_device(): pl.pallas_call(unpack_kernel, out_shape=(local, local, local, jax.ShapeDt...  1.29 us

profile of v6, /device:TPU:0, one launch (start us, length us, event | category | flops | bytes accessed | tf_op | source)
XLA Modules:
  0.0 61.6 jit_solution(14530031099187926664)
XLA Ops:
  0.6 0.0 copy-start.1
  0.6 0.0 copy-start
  0.7 1.7 %pack.1 = bf16[128,32,128]{2,1,0:T(8,128)(2,1)S(1)} custom-call(bf16[1024,128]{1,0:T(8,128)(2,1)} %filter_hbm.1, bf16[1024,128]{1,0:T(8,128)(2,1)} %first_hbm.1, bf16[1024,128]{1,0:T(8,128)(2,1)} %second_hbm.1, bf16[1024,128]{1,0:T(8,128)(2,1)} %gate_hbm.1, bf16[1024,128]{1,0:T(8,128)(2,1)} %upstream_ref.1), custom_call_target="tpu_custom_call" | custom-call | flops 20000000000 | bytes 2400000 | tf_op jit(solution)/shard_map/pack/pallas_call | solution.py:278
  2.4 30.0 %all_to_all.10.in_ref = bf16[128,32,128]{2,1,0:T(8,128)(2,1)S(1)} all-to-all(bf16[128,32,128]{2,1,0:T(8,128)(2,1)S(1)} %pack.1), channel_id=1, replica_groups=mesh['ctx'=8,'tp'=8,'dp'=2] {'ctx','tp','dp'}, dimensions={0} | all-to-all | bytes 2097152 | tf_op jit(solution)/shard_map/all_to_all | solution.py:270
  32.4 0.0 copy-done.1
  32.4 0.0 copy-done
  32.4 0.0 copy-start.2
  32.4 0.0 copy-start.3
  32.4 4.9 %convolve.1 = bf16[128,32,128]{2,1,0:T(8,128)(2,1)S(1)} custom-call(bf16[128,32,128]{2,1,0:T(8,128)(2,1)S(1)} %all_to_all.10.in_ref, bf16[1024,2560]{1,0:T(8,128)(2,1)S(1)} %copy-done, f32[1024,512]{1,0:T(8,128)S(1)} %copy-done.1), custom_call_target="tpu_custom_call" | custom-call | tf_op jit(solution)/shard_map/convolve/pallas_call | solution.py:292
  37.3 23.0 %all_to_all.11.in_ref = bf16[128,32,128]{2,1,0:T(8,128)(2,1)S(1)} all-to-all(bf16[128,32,128]{2,1,0:T(8,128)(2,1)S(1)} %convolve.1), channel_id=1, replica_groups=mesh['ctx'=8,'tp'=8,'dp'=2] {'ctx','tp','dp'}, dimensions={0} | all-to-all | bytes 2097152 | tf_op jit(solution)/shard_map/all_to_all | solution.py:270
  60.3 0.0 copy-done.2
  60.3 0.0 copy-done.3
  60.3 1.3 %unpack.1 = (bf16[1024,128]{1,0:T(8,128)(2,1)}, bf16[1024,128]{1,0:T(8,128)(2,1)}, bf16[1024,128]{1,0:T(8,128)(2,1)}, f32[1024,128]{1,0:T(8,128)}) custom-call(bf16[128,32,128]{2,1,0:T(8,128)(2,1)S(1)} %all_to_all.11.in_ref, bf16[1024,128]{1,0:T(8,128)(2,1)S(1)} %copy-done.3, bf16[1024,128]{1,0:T(8,128)(2,1)S(1)} %copy-done.2), custom_call_target="tpu_custom_call" | custom-call | tf_op jit(solution)/shard_map/unpack/pallas_call | solution.py:302
Async XLA Ops:
  0.6 31.7 %copy-start.1 = (f32[1024,512]{1,0:T(8,128)S(1)}, f32[1024,512]{1,0:T(8,128)}, u32[]{:S(2)}) copy-start(f32[1024,512]{1,0:T(8,128)} %constant.5.clone.twist_ref) | copy-start | bytes 6291460
  0.6 31.7 %copy-start = (bf16[1024,2560]{1,0:T(8,128)(2,1)S(1)}, bf16[1024,2560]{1,0:T(8,128)(2,1)}, u32[]{:S(2)}) copy-start(bf16[1024,2560]{1,0:T(8,128)(2,1)} %constant.4.clone.table_ref) | copy-start | bytes 15728644
  32.4 27.9 %copy-start.2 = (bf16[1024,128]{1,0:T(8,128)(2,1)S(1)}, bf16[1024,128]{1,0:T(8,128)(2,1)}, u32[]{:S(2)}) copy-start(bf16[1024,128]{1,0:T(8,128)(2,1)} %upstream_ref.1) | copy-start | bytes 786436
  32.4 27.9 %copy-start.3 = (bf16[1024,128]{1,0:T(8,128)(2,1)S(1)}, bf16[1024,128]{1,0:T(8,128)(2,1)}, u32[]{:S(2)}) copy-start(bf16[1024,128]{1,0:T(8,128)(2,1)} %gate_ref.1) | copy-start | bytes 786436

commit v7 on v3

--- a/solution.py
+++ b/solution.py
@@ -229,7 +229,8 @@
 
     for pair in range(2):
         lay_out(pair)
-        begin(0, pair)
+        for double in range(STEPS // 2):
+            begin(double, pair)
     for turn in range(1, STEPS + 3):
         if 0 <= turn - 3 < STEPS:
             store(turn - 3, results.pop(turn - 3))
@@ -240,9 +241,6 @@
             results[turn - 2] = multiply(spectra.pop(turn - 2))
         if 0 <= turn - 1 < STEPS:
             spectra[turn - 1] = second_factor(turn - 1, turned.pop(turn - 1))
-        if turn % 2 and turn + 1 < STEPS:
-            for pair in range(2):
-                begin((turn + 1) // 2, pair)
 
     for part in range(HALF // step):
         even, odd = way_back(part, slice(early, FIRST))

time: 61.7 us -> 61.8 us (level)
  no operation moved by 1% of the time
where the time goes in v7:
time: 61.8 us; the launch traced here: 61.7 us
  blocking collectives  53 us (86%)
  Pallas kernels  7.95 us (13%)
  between operations  0.67 us (1%)
    all_to_all x2, blocking collectives, exchange(): return lax.all_to_all(pieces, AXES, split_axis=0, concat_axis=0, tiled=True)  53 us
    pallas_call x1, Pallas kernels, on_device(): pl.pallas_call(convolve_kernel, out_shape=pieces, in_specs=[vmem()] * 3,...  4.97 us
    pallas_call x1, Pallas kernels, on_device(): pl.pallas_call(pack_kernel, out_shape=pieces, in_specs=[hbm()] * 5, out_s...  1.7 us
    pallas_call x1, Pallas kernels, on_device(): pl.pallas_call(unpack_kernel, out_shape=(local, local, local, jax.ShapeDt...  1.29 us

profile of v7, /device:TPU:0, one launch (start us, length us, event | category | flops | bytes accessed | tf_op | source)
XLA Modules:
  0.0 61.7 jit_solution(7318476930590401221)
XLA Ops:
  0.6 0.0 copy-start.1
  0.6 0.0 copy-start
  0.7 1.7 %pack.1 = bf16[128,32,128]{2,1,0:T(8,128)(2,1)S(1)} custom-call(bf16[1024,128]{1,0:T(8,128)(2,1)} %filter_hbm.1, bf16[1024,128]{1,0:T(8,128)(2,1)} %first_hbm.1, bf16[1024,128]{1,0:T(8,128)(2,1)} %second_hbm.1, bf16[1024,128]{1,0:T(8,128)(2,1)} %gate_hbm.1, bf16[1024,128]{1,0:T(8,128)(2,1)} %upstream_ref.1), custom_call_target="tpu_custom_call" | custom-call | flops 20000000000 | bytes 2400000 | tf_op jit(solution)/shard_map/pack/pallas_call | solution.py:275
  2.4 30.0 %all_to_all.10.in_ref = bf16[128,32,128]{2,1,0:T(8,128)(2,1)S(1)} all-to-all(bf16[128,32,128]{2,1,0:T(8,128)(2,1)S(1)} %pack.1), channel_id=1, replica_groups=mesh['ctx'=8,'tp'=8,'dp'=2] {'ctx','tp','dp'}, dimensions={0} | all-to-all | bytes 2097152 | tf_op jit(solution)/shard_map/all_to_all | solution.py:267
  32.4 0.0 copy-done.1
  32.4 0.0 copy-done
  32.4 0.0 copy-start.2
  32.4 0.0 copy-start.3
  32.4 5.0 %convolve.1 = bf16[128,32,128]{2,1,0:T(8,128)(2,1)S(1)} custom-call(bf16[128,32,128]{2,1,0:T(8,128)(2,1)S(1)} %all_to_all.10.in_ref, bf16[1024,2560]{1,0:T(8,128)(2,1)S(1)} %copy-done, f32[1024,512]{1,0:T(8,128)S(1)} %copy-done.1), custom_call_target="tpu_custom_call" | custom-call | tf_op jit(solution)/shard_map/convolve/pallas_call | solution.py:289
  37.4 23.0 %all_to_all.11.in_ref = bf16[128,32,128]{2,1,0:T(8,128)(2,1)S(1)} all-to-all(bf16[128,32,128]{2,1,0:T(8,128)(2,1)S(1)} %convolve.1), channel_id=1, replica_groups=mesh['ctx'=8,'tp'=8,'dp'=2] {'ctx','tp','dp'}, dimensions={0} | all-to-all | bytes 2097152 | tf_op jit(solution)/shard_map/all_to_all | solution.py:267
  60.4 0.0 copy-done.2
  60.4 0.0 copy-done.3
  60.4 1.3 %unpack.1 = (bf16[1024,128]{1,0:T(8,128)(2,1)}, bf16[1024,128]{1,0:T(8,128)(2,1)}, bf16[1024,128]{1,0:T(8,128)(2,1)}, f32[1024,128]{1,0:T(8,128)}) custom-call(bf16[128,32,128]{2,1,0:T(8,128)(2,1)S(1)} %all_to_all.11.in_ref, bf16[1024,128]{1,0:T(8,128)(2,1)S(1)} %copy-done.3, bf16[1024,128]{1,0:T(8,128)(2,1)S(1)} %copy-done.2), custom_call_target="tpu_custom_call" | custom-call | tf_op jit(solution)/shard_map/unpack/pallas_call | solution.py:299
Async XLA Ops:
  0.6 31.7 %copy-start.1 = (f32[1024,512]{1,0:T(8,128)S(1)}, f32[1024,512]{1,0:T(8,128)}, u32[]{:S(2)}) copy-start(f32[1024,512]{1,0:T(8,128)} %constant.5.clone.twist_ref) | copy-start | bytes 6291460
  0.6 31.7 %copy-start = (bf16[1024,2560]{1,0:T(8,128)(2,1)S(1)}, bf16[1024,2560]{1,0:T(8,128)(2,1)}, u32[]{:S(2)}) copy-start(bf16[1024,2560]{1,0:T(8,128)(2,1)} %constant.4.clone.table_ref) | copy-start | bytes 15728644
  32.4 28.0 %copy-start.2 = (bf16[1024,128]{1,0:T(8,128)(2,1)S(1)}, bf16[1024,128]{1,0:T(8,128)(2,1)}, u32[]{:S(2)}) copy-start(bf16[1024,128]{1,0:T(8,128)(2,1)} %upstream_ref.1) | copy-start | bytes 786436
  32.4 28.0 %copy-start.3 = (bf16[1024,128]{1,0:T(8,128)(2,1)S(1)}, bf16[1024,128]{1,0:T(8,128)(2,1)}, u32[]{:S(2)}) copy-start(bf16[1024,128]{1,0:T(8,128)(2,1)} %gate_ref.1) | copy-start | bytes 786436
